TPU v7x, 32 devices: a whole 2x2x4 slice. The times are simulated.
32 devices in a mesh: groups: 2 (over x), gx: 8 (over z, y), gy: 2 (over core).
Axes of the slice: x: 2, y: 2, z: 4, core: 2. Of those that a mesh axis runs over, the one named last changes fastest.
Arguments:
- level_set: float32 [512, 128, 128], P(('groups', 'gx'), 'gy'), parts along dimension 0, may hold values from -5 to 5
- normal_speed: float32 [512, 128, 128], P(('groups', 'gx'), 'gy'), parts along dimension 0, may hold values from -1 to 1
- band_tiles: int32 [32, 8], P(('groups', 'gx'), 'gy'), parts along dimension 0, may hold values from 0 to 1, as said below
Outputs:
- surface: float32 [512, 128, 128], P(('groups', 'gx'), 'gy'), parts along dimension 0
There are 2 independent parts, one for each index of `groups`. A program takes and returns all parts, laid end to end along the dimension named above; each array names one. Nothing has to cross between parts.
Inputs may be any that keep to these rules, and one draw needn't show every extreme that they name: `band_tiles`: in each aligned block of four bricks along gx with the same gy index exactly 12 tiles are band tiles, each aligned pair of bricks in the block holds an even number of them, and one brick of every block has all 8 of its tiles in the band.
All inputs are finite; a program needn't handle non-finite values.
Results may differ from a plain program's by a relative error of at most 0.0003.
Values sent between devices are 32-bit elements; how exact they have to be, the bound alone decides.
A program may use at most 64 MiB of HBM per device.

v0:
```python
import jax
import jax.numpy as jnp
from jax import lax
from jax.sharding import PartitionSpec as P

TILE = 16
RK_STEPS = 2
REINIT = 12


TIME_STEP = 0.25
REINIT_STEP = 0.3
WENO_EPS = 1e-06


def extended(block, sides, width):
    for axis, dim in sides:
        count = lax.axis_size(axis)
        forward = [(i, i + 1) for i in range(count - 1)]
        backward = [(target, source) for source, target in forward]
        low = lax.ppermute(
            lax.slice_in_dim(block, block.shape[dim] - width, None, axis=dim), axis, forward
        )
        high = lax.ppermute(lax.slice_in_dim(block, 0, width, axis=dim), axis, backward)
        block = jnp.concatenate([low, block, high], axis=dim)
    return block


def weno_blend(far_left, near_left, center, near_right, far_right):
    smooth_one = (
        13.0 / 12.0 * (far_left - 2.0 * near_left + center) ** 2
        + 0.25 * (far_left - 4.0 * near_left + 3.0 * center) ** 2
    )
    smooth_two = (
        13.0 / 12.0 * (near_left - 2.0 * center + near_right) ** 2
        + 0.25 * (near_left - near_right) ** 2
    )
    smooth_three = (
        13.0 / 12.0 * (center - 2.0 * near_right + far_right) ** 2
        + 0.25 * (3.0 * center - 4.0 * near_right + far_right) ** 2
    )
    weight_one = 0.1 / (WENO_EPS + smooth_one) ** 2
    weight_two = 0.6 / (WENO_EPS + smooth_two) ** 2
    weight_three = 0.3 / (WENO_EPS + smooth_three) ** 2
    stencil_one = far_left / 3.0 - 7.0 * near_left / 6.0 + 11.0 * center / 6.0
    stencil_two = -near_left / 6.0 + 5.0 * center / 6.0 + near_right / 3.0
    stencil_three = center / 3.0 + 5.0 * near_right / 6.0 - far_right / 6.0
    total = weight_one * stencil_one + weight_two * stencil_two + weight_three * stencil_three
    return total / (weight_one + weight_two + weight_three)


def evolution_rate(padded, velocity):
    extent = velocity.shape
    upwind_pos = jnp.zeros(extent, jnp.float32)
    upwind_neg = jnp.zeros(extent, jnp.float32)
    for direction in range(3):
        cropped = padded
        for crosswise in range(3):
            if crosswise != direction:
                cropped = lax.slice_in_dim(cropped, 3, 3 + extent[crosswise], axis=crosswise)
        length = extent[direction]
        increments = lax.slice_in_dim(cropped, 1, length + 6, axis=direction) - lax.slice_in_dim(
            cropped, 0, length + 5, axis=direction
        )
        shifted = [
            lax.slice_in_dim(increments, offset, offset + length, axis=direction)
            for offset in range(6)
        ]
        behind = weno_blend(shifted[0], shifted[1], shifted[2], shifted[3], shifted[4])
        forward = weno_blend(shifted[5], shifted[4], shifted[3], shifted[2], shifted[1])
        upwind_pos = upwind_pos + jnp.maximum(
            jnp.maximum(behind, 0.0) ** 2, jnp.minimum(forward, 0.0) ** 2
        )
        upwind_neg = upwind_neg + jnp.maximum(
            jnp.minimum(behind, 0.0) ** 2, jnp.maximum(forward, 0.0) ** 2
        )
    magnitude = jnp.where(velocity > 0.0, jnp.sqrt(upwind_pos), jnp.sqrt(upwind_neg))
    return velocity * magnitude


def reinitialize(tile_stack):
    signum = tile_stack / jnp.sqrt(tile_stack * tile_stack + 1.0)

    def one_sweep(iteration, current):
        upwind_pos = jnp.zeros(current.shape, current.dtype)
        upwind_neg = jnp.zeros(current.shape, current.dtype)
        for direction in (1, 2, 3):
            widths = [(0, 0), (0, 0), (0, 0), (0, 0)]
            widths[direction] = (1, 1)
            padded = jnp.pad(current, widths, mode="edge")
            length = current.shape[direction]
            behind = current - lax.slice_in_dim(padded, 0, length, axis=direction)
            forward = lax.slice_in_dim(padded, 2, length + 2, axis=direction) - current
            upwind_pos = upwind_pos + jnp.maximum(
                jnp.maximum(behind, 0.0) ** 2, jnp.minimum(forward, 0.0) ** 2
            )
            upwind_neg = upwind_neg + jnp.maximum(
                jnp.minimum(behind, 0.0) ** 2, jnp.maximum(forward, 0.0) ** 2
            )
        magnitude = jnp.where(tile_stack > 0.0, jnp.sqrt(upwind_pos), jnp.sqrt(upwind_neg))
        return current - REINIT_STEP * signum * (magnitude - 1.0)

    return lax.fori_loop(0, REINIT, one_sweep, tile_stack)


def pad_depth(field_now):
    return jnp.pad(field_now, ((0, 0), (0, 0), (3, 3)))


def body(level_set, normal_speed, band_tiles):
    row_count, col_count, depth_cells = level_set.shape
    surface = level_set

    def section_rate(field_now):
        padded = extended(field_now, (("gx", 0), ("gy", 1)), 3)
        return evolution_rate(pad_depth(padded), normal_speed)

    for advance in range(RK_STEPS):
        halfway = surface - TIME_STEP * section_rate(surface)
        surface = 0.5 * surface + 0.5 * (halfway - TIME_STEP * section_rate(halfway))
    tiles_down = row_count // TILE
    tiles_wide = col_count // TILE
    slot_count = tiles_down * tiles_wide
    tile_stack = surface.reshape(tiles_down, TILE, tiles_wide, TILE, depth_cells).transpose(
        0, 2, 1, 3, 4
    )
    tile_stack = tile_stack.reshape(slot_count, TILE, TILE, depth_cells)
    in_band = band_tiles.reshape(slot_count)
    finished_tiles = reinitialize(tile_stack)
    merged = jnp.where(in_band[:, None, None, None] > 0, finished_tiles, tile_stack)
    merged = merged.reshape(tiles_down, tiles_wide, TILE, TILE, depth_cells).transpose(
        0, 2, 1, 3, 4
    )
    return merged.reshape(row_count, col_count, depth_cells)


def solution(mesh):
    return jax.shard_map(
        body,
        mesh=mesh,
        in_specs=(
            P(("groups", "gx"), "gy", None),
            P(("groups", "gx"), "gy", None),
            P(("groups", "gx"), "gy"),
        ),
        out_specs=P(("groups", "gx"), "gy", None),
        check_vma=False,
    )
```

profile of v0, /device:TPU:0, one launch (start us, length us, event | category | flops | bytes accessed | tf_op | source)
XLA Modules:
  0.0 174.4 jit_solution(5693646805175199717)
XLA Ops:
  0.0 1.0 fusion.17
  1.0 4.9 %collective-permute-start = (f32[3,64,128]{2,1,0:T(8,128)S(1)}, f32[3,64,128]{2,1,0:T(8,128)S(1)}, u32[]{:S(2)}, u32[]{:S(2)}) collective-permute-start(f32[3,64,128]{2,1,0:T(8,128)S(1)} %get-tuple-element.90), channel_id=1, source_target_pairs={{0,2},{2,4},{4,6},{6,8},{8,10},{10,12},{12,14},{1,3},{3,5},{5,7},{... | collective-permute-start | bytes 294920 | tf_op jit(solution)/shard_map/ppermute | solution.py:21
  5.8 1.3 collective-permute-start.1
  7.1 0.9 collective-permute-done
  8.0 1.3 constant_dynamic-update-slice_fusion.1
  9.4 3.0 %collective-permute-done.1 = f32[3,64,128]{2,1,0:T(8,128)S(1)} collective-permute-done((f32[3,64,128]{2,1,0:T(8,128)S(1)}, f32[3,64,128]{2,1,0:T(8,128)S(1)}, u32[]{:S(2)}, u32[]{:S(2)}) %collective-permute-start.1) | collective-permute-done | bytes 98336 | tf_op jit(solution)/shard_map/ppermute | solution.py:24
  12.4 1.3 collective-permute-start.3
  13.7 3.0 %collective-permute-start.2 = (f32[38,3,128]{2,1,0:T(4,128)S(1)}, f32[38,3,128]{2,1,0:T(4,128)S(1)}, u32[]{:S(2)}, u32[]{:S(2)}) collective-permute-start(f32[38,3,128]{2,1,0:T(4,128)S(1)} %get-tuple-element.81), channel_id=1, source_target_pairs={{0,1},{2,3},{4,5},{6,7},{8,9},{10,11},{12,13},{14,15},{16,17},{18,... | collective-permute-start | bytes 175112 | tf_op jit(solution)/shard_map/ppermute | solution.py:21
  16.8 0.8 collective-permute-done.2
  17.8 1.1 fusion.6
  19.1 1.1 copy-done
  20.5 15.8 %multiply_subtract_fusion.2 = f32[32,64,128]{2,1,0:T(8,128)S(1)} fusion(f32[32,64,128]{2,1,0:T(8,128)S(1)} %copy-done.1, f32[32,64,128]{2,1,0:T(8,128)S(1)} %copy-done, f32[32,64,133]{2,1,0:T(8,128)S(1)} %fusion.6, f32[32,69,128]{2,1,0:T(8,128)S(1)} %slice_subtract_fusion.7, f32[37,64,128]{2,1,0:T(8,128)S(1)} %slice_subtract_fusion.3), kind=kLoop, calls=%fused_computation.44 | loop fusion | flops 107741184 | bytes 22020096 | tf_op jit(solution)/shard_map/sub | solution.py:119
  36.3 1.3 collective-permute-start.5
  37.6 5.0 %collective-permute-start.4 = (f32[3,64,128]{2,1,0:T(8,128)S(1)}, f32[3,64,128]{2,1,0:T(8,128)S(1)}, u32[]{:S(2)}, u32[]{:S(2)}) collective-permute-start(f32[3,64,128]{2,1,0:T(8,128)S(1)} %get-tuple-element.87), channel_id=1, source_target_pairs={{0,2},{2,4},{4,6},{6,8},{8,10},{10,12},{12,14},{1,3},{3,5},{5,7},{... | collective-permute-start | bytes 294920 | tf_op jit(solution)/shard_map/ppermute | solution.py:21
  42.6 1.4 collective-permute-done.5
  43.9 2.3 %collective-permute-done.4 = f32[3,64,128]{2,1,0:T(8,128)S(1)} collective-permute-done((f32[3,64,128]{2,1,0:T(8,128)S(1)}, f32[3,64,128]{2,1,0:T(8,128)S(1)}, u32[]{:S(2)}, u32[]{:S(2)}) %collective-permute-start.4) | collective-permute-done | bytes 98336 | tf_op jit(solution)/shard_map/ppermute | solution.py:21
  46.3 1.3 collective-permute-start.7
  47.6 3.0 %collective-permute-start.6 = (f32[38,3,128]{2,1,0:T(4,128)S(1)}, f32[38,3,128]{2,1,0:T(4,128)S(1)}, u32[]{:S(2)}, u32[]{:S(2)}) collective-permute-start(f32[38,3,128]{2,1,0:T(4,128)S(1)} %get-tuple-element.79), channel_id=1, source_target_pairs={{0,1},{2,3},{4,5},{6,7},{8,9},{10,11},{12,13},{14,15},{16,17},{18,... | collective-permute-start | bytes 175112 | tf_op jit(solution)/shard_map/ppermute | solution.py:21
  50.8 0.7 collective-permute-done.6
  51.7 1.1 fusion.7
  52.9 15.9 %broadcast_multiply_fusion = (f32[32,64,128]{2,1,0:T(8,128)S(1)}, f32[32,64,128]{2,1,0:T(8,128)S(1)}) fusion(f32[32,64,128]{2,1,0:T(8,128)S(1)} %copy-done.1, f32[32,64,128]{2,1,0:T(8,128)S(1)} %multiply_subtract_fusion.2, f32[32,64,128]{2,1,0:T(8,128)S(1)} %copy-done, f32[32,64,133]{2,1,0:T(8,128)S(1)} %fusion.7, ...), kind=kLoop, calls=%fused_computation.45 | loop fusion | flops 108265472 | bytes 24117248 | tf_op jit(solution)/shard_map/add | solution.py:120
  68.9 1.3 collective-permute-start.9
  70.2 5.0 %collective-permute-start.8 = (f32[3,64,128]{2,1,0:T(8,128)S(1)}, f32[3,64,128]{2,1,0:T(8,128)S(1)}, u32[]{:S(2)}, u32[]{:S(2)}) collective-permute-start(f32[3,64,128]{2,1,0:T(8,128)S(1)} %get-tuple-element.85), channel_id=1, source_target_pairs={{0,2},{2,4},{4,6},{6,8},{8,10},{10,12},{12,14},{1,3},{3,5},{5,7},{... | collective-permute-start | bytes 294920 | tf_op jit(solution)/shard_map/ppermute | solution.py:21
  75.2 1.4 collective-permute-done.9
  76.5 2.3 %collective-permute-done.8 = f32[3,64,128]{2,1,0:T(8,128)S(1)} collective-permute-done((f32[3,64,128]{2,1,0:T(8,128)S(1)}, f32[3,64,128]{2,1,0:T(8,128)S(1)}, u32[]{:S(2)}, u32[]{:S(2)}) %collective-permute-start.8) | collective-permute-done | bytes 98336 | tf_op jit(solution)/shard_map/ppermute | solution.py:21
  78.8 1.3 collective-permute-start.11
  80.1 3.2 %collective-permute-start.10 = (f32[38,3,128]{2,1,0:T(4,128)S(1)}, f32[38,3,128]{2,1,0:T(4,128)S(1)}, u32[]{:S(2)}, u32[]{:S(2)}) collective-permute-start(f32[38,3,128]{2,1,0:T(4,128)S(1)} %get-tuple-element.77), channel_id=1, source_target_pairs={{0,1},{2,3},{4,5},{6,7},{8,9},{10,11},{12,13},{14,15},{16,17},{18,... | collective-permute-start | bytes 175112 | tf_op jit(solution)/shard_map/ppermute | solution.py:21
  83.6 0.5 collective-permute-done.10
  84.2 1.1 fusion.8
  85.5 15.8 %multiply_subtract_fusion.1 = f32[32,64,128]{2,1,0:T(8,128)S(1)} fusion(f32[32,64,128]{2,1,0:T(8,128)S(1)} %copy-done, f32[32,64,133]{2,1,0:T(8,128)S(1)} %fusion.8, f32[32,69,128]{2,1,0:T(8,128)S(1)} %slice_subtract_fusion.5, f32[37,64,128]{2,1,0:T(8,128)S(1)} %slice_subtract_fusion.1, f32[32,64,128]{2,1,0:T(8,128)S(1)} %get-tuple-element.68), kind=kLoop, calls=%fused_computation.42 | loop fusion | flops 108003328 | bytes 22020096 | tf_op jit(solution)/shard_map/sub | solution.py:119
  101.4 1.3 collective-permute-start.13
  102.7 5.0 %collective-permute-start.12 = (f32[3,64,128]{2,1,0:T(8,128)S(1)}, f32[3,64,128]{2,1,0:T(8,128)S(1)}, u32[]{:S(2)}, u32[]{:S(2)}) collective-permute-start(f32[3,64,128]{2,1,0:T(8,128)S(1)} %get-tuple-element.83), channel_id=1, source_target_pairs={{0,2},{2,4},{4,6},{6,8},{8,10},{10,12},{12,14},{1,3},{3,5},{5,7},{... | collective-permute-start | bytes 294920 | tf_op jit(solution)/shard_map/ppermute | solution.py:21
  107.8 1.3 collective-permute-done.13
  109.1 2.3 %collective-permute-done.12 = f32[3,64,128]{2,1,0:T(8,128)S(1)} collective-permute-done((f32[3,64,128]{2,1,0:T(8,128)S(1)}, f32[3,64,128]{2,1,0:T(8,128)S(1)}, u32[]{:S(2)}, u32[]{:S(2)}) %collective-permute-start.12) | collective-permute-done | bytes 98336 | tf_op jit(solution)/shard_map/ppermute | solution.py:21
  111.4 1.3 collective-permute-start.15
  112.7 3.0 %collective-permute-start.14 = (f32[38,3,128]{2,1,0:T(4,128)S(1)}, f32[38,3,128]{2,1,0:T(4,128)S(1)}, u32[]{:S(2)}, u32[]{:S(2)}) collective-permute-start(f32[38,3,128]{2,1,0:T(4,128)S(1)} %get-tuple-element.75), channel_id=1, source_target_pairs={{0,1},{2,3},{4,5},{6,7},{8,9},{10,11},{12,13},{14,15},{16,17},{18,... | collective-permute-start | bytes 175112 | tf_op jit(solution)/shard_map/ppermute | solution.py:21
  115.9 0.7 collective-permute-done.14
  116.8 1.1 fusion.9
  118.0 15.9 %multiply_add_fusion = f32[32,64,128]{2,1,0:T(8,128)S(1)} fusion(f32[32,64,128]{2,1,0:T(8,128)S(1)} %multiply_subtract_fusion.1, f32[32,64,128]{2,1,0:T(8,128)S(1)} %copy-done, f32[32,64,133]{2,1,0:T(8,128)S(1)} %fusion.9, f32[32,69,128]{2,1,0:T(8,128)S(1)} %slice_subtract_fusion.4, f32[37,64,128]{2,1,0:T(8,128)S(1)} %slice_subtract_fusion, ...), kind=kLoop, calls=%fused_computation.41 | loop fusion | flops 108527616 | bytes 23068672 | tf_op jit(solution)/shard_map/add | solution.py:120
  134.3 38.8 %while.12 = (s32[]{:T(128)}, f32[8,16,16,128]{3,2,1,0:T(8,128)S(1)}, f32[8,16,16,128]{3,2,1,0:T(8,128)S(1)}, f32[8,16,16,128]{3,2,1,0:T(8,128)S(1)}, s32[]{:T(128)}) while((s32[]{:T(128)}, f32[8,16,16,128]{3,2,1,0:T(8,128)S(1)}, f32[8,16,16,128]{3,2,1,0:T(8,128)S(1)}, f32[8,16,16,128]{3,2,1,0:T(8,128)S(1)}, s32[]{:T(128)}) %tuple.47), condition=%wide.region_1.2_spmd, body=%wide.region_0.1_spmd.sunk | while | flops 13631490 | bytes 7127101 | solution.py:103
  134.4 0.4 fusion.21
  134.9 2.7 %multiply_subtract_fusion.4 = f32[8,16,16,128]{3,2,1,0:T(8,128)S(1)} fusion(f32[8,16,16,128]{3,2,1,0:T(8,128)S(1)} %copy.17, f32[8,16,16,1]{3,2,1,0:T(8,128)S(1)} %get-tuple-element.122, f32[8,16,16,1]{3,2,1,0:T(8,128)S(1)} %get-tuple-element.123, f32[8,16,1,128]{3,2,1,0:T(1,128)S(1)} %get-tuple-element.124, ...), kind=kLoop, calls=%fused_computation.12.clone.1 | loop fusion | flops 13631488 | bytes 4472832 | tf_op jit(solution)/shard_map/while/body/eval_jaxpr/sub | solution.py:101
  137.6 0.4 fusion.21
  138.1 2.7 %multiply_subtract_fusion.4 = f32[8,16,16,128]{3,2,1,0:T(8,128)S(1)} fusion(f32[8,16,16,128]{3,2,1,0:T(8,128)S(1)} %copy.17, f32[8,16,16,1]{3,2,1,0:T(8,128)S(1)} %get-tuple-element.122, f32[8,16,16,1]{3,2,1,0:T(8,128)S(1)} %get-tuple-element.123, f32[8,16,1,128]{3,2,1,0:T(1,128)S(1)} %get-tuple-element.124, ...), kind=kLoop, calls=%fused_computation.12.clone.1 | loop fusion | flops 13631488 | bytes 4472832 | tf_op jit(solution)/shard_map/while/body/eval_jaxpr/sub | solution.py:101
  140.9 0.4 fusion.21
  141.3 2.7 %multiply_subtract_fusion.4 = f32[8,16,16,128]{3,2,1,0:T(8,128)S(1)} fusion(f32[8,16,16,128]{3,2,1,0:T(8,128)S(1)} %copy.17, f32[8,16,16,1]{3,2,1,0:T(8,128)S(1)} %get-tuple-element.122, f32[8,16,16,1]{3,2,1,0:T(8,128)S(1)} %get-tuple-element.123, f32[8,16,1,128]{3,2,1,0:T(1,128)S(1)} %get-tuple-element.124, ...), kind=kLoop, calls=%fused_computation.12.clone.1 | loop fusion | flops 13631488 | bytes 4472832 | tf_op jit(solution)/shard_map/while/body/eval_jaxpr/sub | solution.py:101
  144.1 0.4 fusion.21
  144.6 2.7 %multiply_subtract_fusion.4 = f32[8,16,16,128]{3,2,1,0:T(8,128)S(1)} fusion(f32[8,16,16,128]{3,2,1,0:T(8,128)S(1)} %copy.17, f32[8,16,16,1]{3,2,1,0:T(8,128)S(1)} %get-tuple-element.122, f32[8,16,16,1]{3,2,1,0:T(8,128)S(1)} %get-tuple-element.123, f32[8,16,1,128]{3,2,1,0:T(1,128)S(1)} %get-tuple-element.124, ...), kind=kLoop, calls=%fused_computation.12.clone.1 | loop fusion | flops 13631488 | bytes 4472832 | tf_op jit(solution)/shard_map/while/body/eval_jaxpr/sub | solution.py:101
  147.3 0.4 fusion.21
  147.8 2.7 %multiply_subtract_fusion.4 = f32[8,16,16,128]{3,2,1,0:T(8,128)S(1)} fusion(f32[8,16,16,128]{3,2,1,0:T(8,128)S(1)} %copy.17, f32[8,16,16,1]{3,2,1,0:T(8,128)S(1)} %get-tuple-element.122, f32[8,16,16,1]{3,2,1,0:T(8,128)S(1)} %get-tuple-element.123, f32[8,16,1,128]{3,2,1,0:T(1,128)S(1)} %get-tuple-element.124, ...), kind=kLoop, calls=%fused_computation.12.clone.1 | loop fusion | flops 13631488 | bytes 4472832 | tf_op jit(solution)/shard_map/while/body/eval_jaxpr/sub | solution.py:101
  150.6 0.4 fusion.21
  151.0 2.7 %multiply_subtract_fusion.4 = f32[8,16,16,128]{3,2,1,0:T(8,128)S(1)} fusion(f32[8,16,16,128]{3,2,1,0:T(8,128)S(1)} %copy.17, f32[8,16,16,1]{3,2,1,0:T(8,128)S(1)} %get-tuple-element.122, f32[8,16,16,1]{3,2,1,0:T(8,128)S(1)} %get-tuple-element.123, f32[8,16,1,128]{3,2,1,0:T(1,128)S(1)} %get-tuple-element.124, ...), kind=kLoop, calls=%fused_computation.12.clone.1 | loop fusion | flops 13631488 | bytes 4472832 | tf_op jit(solution)/shard_map/while/body/eval_jaxpr/sub | solution.py:101
  153.8 0.4 fusion.21
  154.3 2.7 %multiply_subtract_fusion.4 = f32[8,16,16,128]{3,2,1,0:T(8,128)S(1)} fusion(f32[8,16,16,128]{3,2,1,0:T(8,128)S(1)} %copy.17, f32[8,16,16,1]{3,2,1,0:T(8,128)S(1)} %get-tuple-element.122, f32[8,16,16,1]{3,2,1,0:T(8,128)S(1)} %get-tuple-element.123, f32[8,16,1,128]{3,2,1,0:T(1,128)S(1)} %get-tuple-element.124, ...), kind=kLoop, calls=%fused_computation.12.clone.1 | loop fusion | flops 13631488 | bytes 4472832 | tf_op jit(solution)/shard_map/while/body/eval_jaxpr/sub | solution.py:101
  157.0 0.4 fusion.21
  157.5 2.7 %multiply_subtract_fusion.4 = f32[8,16,16,128]{3,2,1,0:T(8,128)S(1)} fusion(f32[8,16,16,128]{3,2,1,0:T(8,128)S(1)} %copy.17, f32[8,16,16,1]{3,2,1,0:T(8,128)S(1)} %get-tuple-element.122, f32[8,16,16,1]{3,2,1,0:T(8,128)S(1)} %get-tuple-element.123, f32[8,16,1,128]{3,2,1,0:T(1,128)S(1)} %get-tuple-element.124, ...), kind=kLoop, calls=%fused_computation.12.clone.1 | loop fusion | flops 13631488 | bytes 4472832 | tf_op jit(solution)/shard_map/while/body/eval_jaxpr/sub | solution.py:101
  160.3 0.4 fusion.21
  160.7 2.7 %multiply_subtract_fusion.4 = f32[8,16,16,128]{3,2,1,0:T(8,128)S(1)} fusion(f32[8,16,16,128]{3,2,1,0:T(8,128)S(1)} %copy.17, f32[8,16,16,1]{3,2,1,0:T(8,128)S(1)} %get-tuple-element.122, f32[8,16,16,1]{3,2,1,0:T(8,128)S(1)} %get-tuple-element.123, f32[8,16,1,128]{3,2,1,0:T(1,128)S(1)} %get-tuple-element.124, ...), kind=kLoop, calls=%fused_computation.12.clone.1 | loop fusion | flops 13631488 | bytes 4472832 | tf_op jit(solution)/shard_map/while/body/eval_jaxpr/sub | solution.py:101
  163.5 0.4 fusion.21
  164.0 2.7 %multiply_subtract_fusion.4 = f32[8,16,16,128]{3,2,1,0:T(8,128)S(1)} fusion(f32[8,16,16,128]{3,2,1,0:T(8,128)S(1)} %copy.17, f32[8,16,16,1]{3,2,1,0:T(8,128)S(1)} %get-tuple-element.122, f32[8,16,16,1]{3,2,1,0:T(8,128)S(1)} %get-tuple-element.123, f32[8,16,1,128]{3,2,1,0:T(1,128)S(1)} %get-tuple-element.124, ...), kind=kLoop, calls=%fused_computation.12.clone.1 | loop fusion | flops 13631488 | bytes 4472832 | tf_op jit(solution)/shard_map/while/body/eval_jaxpr/sub | solution.py:101
  166.7 0.4 fusion.21
  167.2 2.7 %multiply_subtract_fusion.4 = f32[8,16,16,128]{3,2,1,0:T(8,128)S(1)} fusion(f32[8,16,16,128]{3,2,1,0:T(8,128)S(1)} %copy.17, f32[8,16,16,1]{3,2,1,0:T(8,128)S(1)} %get-tuple-element.122, f32[8,16,16,1]{3,2,1,0:T(8,128)S(1)} %get-tuple-element.123, f32[8,16,1,128]{3,2,1,0:T(1,128)S(1)} %get-tuple-element.124, ...), kind=kLoop, calls=%fused_computation.12.clone.1 | loop fusion | flops 13631488 | bytes 4472832 | tf_op jit(solution)/shard_map/while/body/eval_jaxpr/sub | solution.py:101
  170.5 2.7 %multiply_subtract_fusion.4 = f32[8,16,16,128]{3,2,1,0:T(8,128)S(1)} fusion(f32[8,16,16,128]{3,2,1,0:T(8,128)S(1)} %copy.17, f32[8,16,16,1]{3,2,1,0:T(8,128)S(1)} %get-tuple-element.122, f32[8,16,16,1]{3,2,1,0:T(8,128)S(1)} %get-tuple-element.123, f32[8,16,1,128]{3,2,1,0:T(1,128)S(1)} %get-tuple-element.124, ...), kind=kLoop, calls=%fused_computation.12.clone.1 | loop fusion | flops 13631488 | bytes 4472832 | tf_op jit(solution)/shard_map/while/body/eval_jaxpr/sub | solution.py:101
  173.3 1.1 copy.5
  (76 shorter events, 5.3 us)
Async XLA Ops:
  1.0 7.1 %collective-permute-start = (f32[3,64,128]{2,1,0:T(8,128)S(1)}, f32[3,64,128]{2,1,0:T(8,128)S(1)}, u32[]{:S(2)}, u32[]{:S(2)}) collective-permute-start(f32[3,64,128]{2,1,0:T(8,128)S(1)} %get-tuple-element.90), channel_id=1, source_target_pairs={{0,2},{2,4},{4,6},{6,8},{8,10},{10,12},{12,14},{1,3},{3,5},{5,7},{... | collective-permute-start | bytes 294920 | tf_op jit(solution)/shard_map/ppermute | solution.py:21
  5.8 6.5 %collective-permute-start.1 = (f32[3,64,128]{2,1,0:T(8,128)S(1)}, f32[3,64,128]{2,1,0:T(8,128)S(1)}, u32[]{:S(2)}, u32[]{:S(2)}) collective-permute-start(f32[3,64,128]{2,1,0:T(8,128)S(1)} %get-tuple-element.89), channel_id=1, source_target_pairs={{2,0},{4,2},{6,4},{8,6},{10,8},{12,10},{14,12},{3,1},{5,3},{7,5},{... | collective-permute-start | bytes 294920 | tf_op jit(solution)/shard_map/ppermute | solution.py:24
  12.4 4.4 %collective-permute-start.3 = (f32[38,3,128]{2,1,0:T(4,128)S(1)}, f32[38,3,128]{2,1,0:T(4,128)S(1)}, u32[]{:S(2)}, u32[]{:S(2)}) collective-permute-start(f32[38,3,128]{2,1,0:T(4,128)S(1)} %get-tuple-element.82), channel_id=1, source_target_pairs={{1,0},{3,2},{5,4},{7,6},{9,8},{11,10},{13,12},{15,14},{17,16},{19,... | collective-permute-start | bytes 175112 | tf_op jit(solution)/shard_map/ppermute | solution.py:24
  13.7 3.9 %collective-permute-start.2 = (f32[38,3,128]{2,1,0:T(4,128)S(1)}, f32[38,3,128]{2,1,0:T(4,128)S(1)}, u32[]{:S(2)}, u32[]{:S(2)}) collective-permute-start(f32[38,3,128]{2,1,0:T(4,128)S(1)} %get-tuple-element.81), channel_id=1, source_target_pairs={{0,1},{2,3},{4,5},{6,7},{8,9},{10,11},{12,13},{14,15},{16,17},{18,... | collective-permute-start | bytes 175112 | tf_op jit(solution)/shard_map/ppermute | solution.py:21
  19.0 1.2 copy-start
  19.0 1.5 copy-start.1
  36.3 7.6 %collective-permute-start.5 = (f32[3,64,128]{2,1,0:T(8,128)S(1)}, f32[3,64,128]{2,1,0:T(8,128)S(1)}, u32[]{:S(2)}, u32[]{:S(2)}) collective-permute-start(f32[3,64,128]{2,1,0:T(8,128)S(1)} %get-tuple-element.88), channel_id=1, source_target_pairs={{2,0},{4,2},{6,4},{8,6},{10,8},{12,10},{14,12},{3,1},{5,3},{7,5},{... | collective-permute-start | bytes 294920 | tf_op jit(solution)/shard_map/ppermute | solution.py:24
  37.6 8.6 %collective-permute-start.4 = (f32[3,64,128]{2,1,0:T(8,128)S(1)}, f32[3,64,128]{2,1,0:T(8,128)S(1)}, u32[]{:S(2)}, u32[]{:S(2)}) collective-permute-start(f32[3,64,128]{2,1,0:T(8,128)S(1)} %get-tuple-element.87), channel_id=1, source_target_pairs={{0,2},{2,4},{4,6},{6,8},{8,10},{10,12},{12,14},{1,3},{3,5},{5,7},{... | collective-permute-start | bytes 294920 | tf_op jit(solution)/shard_map/ppermute | solution.py:21
  46.3 4.5 %collective-permute-start.7 = (f32[38,3,128]{2,1,0:T(4,128)S(1)}, f32[38,3,128]{2,1,0:T(4,128)S(1)}, u32[]{:S(2)}, u32[]{:S(2)}) collective-permute-start(f32[38,3,128]{2,1,0:T(4,128)S(1)} %get-tuple-element.80), channel_id=1, source_target_pairs={{1,0},{3,2},{5,4},{7,6},{9,8},{11,10},{13,12},{15,14},{17,16},{19,... | collective-permute-start | bytes 175112 | tf_op jit(solution)/shard_map/ppermute | solution.py:24
  47.6 3.9 %collective-permute-start.6 = (f32[38,3,128]{2,1,0:T(4,128)S(1)}, f32[38,3,128]{2,1,0:T(4,128)S(1)}, u32[]{:S(2)}, u32[]{:S(2)}) collective-permute-start(f32[38,3,128]{2,1,0:T(4,128)S(1)} %get-tuple-element.79), channel_id=1, source_target_pairs={{0,1},{2,3},{4,5},{6,7},{8,9},{10,11},{12,13},{14,15},{16,17},{18,... | collective-permute-start | bytes 175112 | tf_op jit(solution)/shard_map/ppermute | solution.py:21
  68.9 7.7 %collective-permute-start.9 = (f32[3,64,128]{2,1,0:T(8,128)S(1)}, f32[3,64,128]{2,1,0:T(8,128)S(1)}, u32[]{:S(2)}, u32[]{:S(2)}) collective-permute-start(f32[3,64,128]{2,1,0:T(8,128)S(1)} %get-tuple-element.86), channel_id=1, source_target_pairs={{2,0},{4,2},{6,4},{8,6},{10,8},{12,10},{14,12},{3,1},{5,3},{7,5},{... | collective-permute-start | bytes 294920 | tf_op jit(solution)/shard_map/ppermute | solution.py:24
  70.2 8.7 %collective-permute-start.8 = (f32[3,64,128]{2,1,0:T(8,128)S(1)}, f32[3,64,128]{2,1,0:T(8,128)S(1)}, u32[]{:S(2)}, u32[]{:S(2)}) collective-permute-start(f32[3,64,128]{2,1,0:T(8,128)S(1)} %get-tuple-element.85), channel_id=1, source_target_pairs={{0,2},{2,4},{4,6},{6,8},{8,10},{10,12},{12,14},{1,3},{3,5},{5,7},{... | collective-permute-start | bytes 294920 | tf_op jit(solution)/shard_map/ppermute | solution.py:21
  78.8 4.7 %collective-permute-start.11 = (f32[38,3,128]{2,1,0:T(4,128)S(1)}, f32[38,3,128]{2,1,0:T(4,128)S(1)}, u32[]{:S(2)}, u32[]{:S(2)}) collective-permute-start(f32[38,3,128]{2,1,0:T(4,128)S(1)} %get-tuple-element.78), channel_id=1, source_target_pairs={{1,0},{3,2},{5,4},{7,6},{9,8},{11,10},{13,12},{15,14},{17,16},{19,... | collective-permute-start | bytes 175112 | tf_op jit(solution)/shard_map/ppermute | solution.py:24
  80.1 3.9 %collective-permute-start.10 = (f32[38,3,128]{2,1,0:T(4,128)S(1)}, f32[38,3,128]{2,1,0:T(4,128)S(1)}, u32[]{:S(2)}, u32[]{:S(2)}) collective-permute-start(f32[38,3,128]{2,1,0:T(4,128)S(1)} %get-tuple-element.77), channel_id=1, source_target_pairs={{0,1},{2,3},{4,5},{6,7},{8,9},{10,11},{12,13},{14,15},{16,17},{18,... | collective-permute-start | bytes 175112 | tf_op jit(solution)/shard_map/ppermute | solution.py:21
  85.5 22.2 %copy-start.2 = (s32[2,4]{1,0:T(2,128)S(1)}, s32[2,4]{1,0:T(2,128)}, u32[]{:S(2)}) copy-start(s32[2,4]{1,0:T(2,128)} %param.7) | copy-start | bytes 100
  101.4 7.7 %collective-permute-start.13 = (f32[3,64,128]{2,1,0:T(8,128)S(1)}, f32[3,64,128]{2,1,0:T(8,128)S(1)}, u32[]{:S(2)}, u32[]{:S(2)}) collective-permute-start(f32[3,64,128]{2,1,0:T(8,128)S(1)} %get-tuple-element.84), channel_id=1, source_target_pairs={{2,0},{4,2},{6,4},{8,6},{10,8},{12,10},{14,12},{3,1},{5,3},{7,5},{... | collective-permute-start | bytes 294920 | tf_op jit(solution)/shard_map/ppermute | solution.py:24
  102.7 8.7 %collective-permute-start.12 = (f32[3,64,128]{2,1,0:T(8,128)S(1)}, f32[3,64,128]{2,1,0:T(8,128)S(1)}, u32[]{:S(2)}, u32[]{:S(2)}) collective-permute-start(f32[3,64,128]{2,1,0:T(8,128)S(1)} %get-tuple-element.83), channel_id=1, source_target_pairs={{0,2},{2,4},{4,6},{6,8},{8,10},{10,12},{12,14},{1,3},{3,5},{5,7},{... | collective-permute-start | bytes 294920 | tf_op jit(solution)/shard_map/ppermute | solution.py:21
  111.4 4.5 %collective-permute-start.15 = (f32[38,3,128]{2,1,0:T(4,128)S(1)}, f32[38,3,128]{2,1,0:T(4,128)S(1)}, u32[]{:S(2)}, u32[]{:S(2)}) collective-permute-start(f32[38,3,128]{2,1,0:T(4,128)S(1)} %get-tuple-element.76), channel_id=1, source_target_pairs={{1,0},{3,2},{5,4},{7,6},{9,8},{11,10},{13,12},{15,14},{17,16},{19,... | collective-permute-start | bytes 175112 | tf_op jit(solution)/shard_map/ppermute | solution.py:24
  112.7 3.9 %collective-permute-start.14 = (f32[38,3,128]{2,1,0:T(4,128)S(1)}, f32[38,3,128]{2,1,0:T(4,128)S(1)}, u32[]{:S(2)}, u32[]{:S(2)}) collective-permute-start(f32[38,3,128]{2,1,0:T(4,128)S(1)} %get-tuple-element.75), channel_id=1, source_target_pairs={{0,1},{2,3},{4,5},{6,7},{8,9},{10,11},{12,13},{14,15},{16,17},{18,... | collective-permute-start | bytes 175112 | tf_op jit(solution)/shard_map/ppermute | solution.py:21
where the time goes:
time: 176 us; the launch traced here: 174 us
  other arithmetic  102 us (58%)
  starting transfers between devices  42.5 us (24%)
  waiting for transfers between devices  17.4 us (10%)
  local copies, waits for them, and re-layouts  11.5 us (7%)
    ppermute x8, starting transfers between devices, extended(): lax.ppermute(lax.slice_in_dim(block, block.shape[dim] - width, None, axis...  32.1 us
    sub x12, other arithmetic, one_sweep(): return current - REINIT_STEP * signum * (magnitude - 1.0)  31.9 us
    add x2, other arithmetic, body(): 0.5 * surface + 0.5 * (halfway - TIME_STEP * section_rate(halfway))  31.8 us
    sub x2, other arithmetic, body(): halfway = surface - TIME_STEP * section_rate(surface)  31.6 us
    ppermute x8, waiting for transfers between devices, extended(): lax.ppermute(lax.slice_in_dim(block, block.shape[dim] - width, None, axis...  10.4 us
    ppermute x8, starting transfers between devices, extended(): lax.ppermute(lax.slice_in_dim(block, 0, width, axis=dim), axis, backward)  10.3 us
    ppermute x8, waiting for transfers between devices, extended(): lax.ppermute(lax.slice_in_dim(block, 0, width, axis=dim), axis, backward)  7 us
    slice x36, local copies, waits for them, and re-layouts, one_sweep(): padded = jnp.pad(current, widths, mode='edge')  5.51 us
  transfers between devices with their start and end apart: 16, of which 12 were waited for; matrix products, arithmetic and copies ran while one was open for 1% of the time, Pallas kernels for 0%

commit v1 on v0

v1 whole, which is shorter than its diff:
```python
import functools

import jax
import jax.numpy as jnp
from jax import lax
from jax.experimental import pallas as pl
from jax.experimental.pallas import tpu as pltpu
from jax.sharding import PartitionSpec as P

TILE = 16
RK_STEPS = 2
REINIT = 12
STAGES = 2 * RK_STEPS
GHOST = 3
SCALE = 1.5 ** 0.5
STEP = 0.125
EPS = 0.75e-6
TINY = 1e-37
PITCH = 144
OUT_PITCH = 136
ZPAD = 8
MESH = pl.DeviceIdType.MESH


def rcp(x):
    return pl.reciprocal(x, approx=True)


def root(x):
    return x * lax.rsqrt(jnp.maximum(x, TINY))


def stencil(x, y):
    e = y - x
    f = e * (1.0 / 3.0)
    mid = (e * f) * 2.0 + ((x * y) * 0.5 + EPS)
    left = mid + y * e
    right = mid - x * e
    rm = rcp(mid)
    rl = rcp(left)
    rr = rcp(right)
    b = (rm * rm) * 6.0
    a = rl * rl
    w = rr * rr
    a3 = a * 3.0
    w3 = w * 3.0
    r1 = y + f
    l1 = x - f
    return (
        (a, a3, a * (r1 + f), a3 * r1),
        (b, b * (y - f), b * (x + f)),
        (w, w3, w * (l1 - f), w3 * l1),
    )


def push(state, phi):
    last_phi, last_d, older_d, last_g, left_old, left_new, mid_new = state
    d = phi - last_phi
    g = d - last_d
    left, mid, right = stencil(last_g, g)
    a, a3, ar2, ar1 = left_old
    b, bc2, bc1 = mid_new
    w, w3, wl2, wl1 = right
    c2 = older_d + older_d
    behind = c2 + (ar2 + bc2 + wl1) * rcp(a + b + w3)
    ahead = (wl2 + bc1 + ar1) * rcp(w + b + a3) - c2
    return (phi, d, last_d, g, left_new, left, mid), behind, ahead


def begin(cells):
    p0, p1, p2, p3, p4 = cells
    d1, d2, d3, d4 = p1 - p0, p2 - p1, p3 - p2, p4 - p3
    g1, g2, g3 = d2 - d1, d3 - d2, d4 - d3
    left_a, _, _ = stencil(g1, g2)
    left_b, mid_b, _ = stencil(g2, g3)
    return (p4, d4, d3, g3, left_a, left_b, mid_b)


def upwind(sign, behind, ahead):
    v = jnp.maximum(jnp.maximum(sign * behind, sign * ahead), 0.0)
    return v * v


def advance_kernel(
    rows, cols, n_gx, n_gy,
    level_ref, speed_hbm, out_ref,
    field, speed, sign, acc_y, acc_z, zin, zout, zsign, yface, yhalo,
    send_sem, recv_sem, local_sem,
):
    cells = rows * cols
    pad = GHOST * cols
    span = cells + 2 * pad
    blocks = cells // 128
    groups = blocks // 8
    gx = lax.axis_index("gx")
    gy = lax.axis_index("gy")
    low_x, high_x = gx > 0, gx < n_gx - 1
    low_y, high_y = gy > 0, gy < n_gy - 1
    sides = (
        (low_x, {"gx": gx - 1}), (high_x, {"gx": gx + 1}),
        (low_y, {"gy": gy - 1}), (high_y, {"gy": gy + 1}),
    )

    load_level = pltpu.make_async_copy(level_ref, acc_y, local_sem.at[0])
    load_speed = pltpu.make_async_copy(speed_hbm, speed, local_sem.at[1])
    load_level.start()
    load_speed.start()

    barrier = pltpu.get_barrier_semaphore()
    for there, device in sides:
        @pl.when(there)
        def _():
            pl.semaphore_signal(barrier, inc=1, device_id=device, device_id_type=MESH)

    zero = jnp.zeros((pad, 128), jnp.float32)
    for stage in range(STAGES):
        @pl.when(jnp.logical_not(low_x))
        def _():
            field[pl.ds(stage * span, pad)] = zero

        @pl.when(jnp.logical_not(high_x))
        def _():
            field[pl.ds(stage * span + pad + cells, pad)] = zero

        @pl.when(jnp.logical_not(low_y))
        def _():
            yhalo[pl.ds((stage * 2) * GHOST * rows, GHOST * rows)] = zero[: GHOST * rows]

        @pl.when(jnp.logical_not(high_y))
        def _():
            yhalo[pl.ds((stage * 2 + 1) * GHOST * rows, GHOST * rows)] = zero[: GHOST * rows]

    for block in range(blocks):
        zin[pl.ds(block * PITCH, ZPAD)] = jnp.zeros((ZPAD, 128), jnp.float32)
        zin[pl.ds(block * PITCH + ZPAD + 128, ZPAD)] = jnp.zeros((ZPAD, 128), jnp.float32)

    load_speed.wait()

    def signs(block, carry):
        at = pl.multiple_of(block * 128, 128)
        v = jnp.where(speed[pl.ds(at, 128)] > 0.0, 1.0, -1.0)
        sign[pl.ds(at, 128)] = v
        zsign[pl.ds(pl.multiple_of(block * OUT_PITCH, 8), 128)] = v.T
        return carry

    lax.fori_loop(0, blocks, signs, 0)
    load_level.wait()

    def scaled(block, carry):
        at = pl.multiple_of(block * 128, 128)
        field[pl.ds(pad + at, 128)] = acc_y[pl.ds(at, 128)] * SCALE
        return carry

    lax.fori_loop(0, blocks, scaled, 0)

    there_count = sum(there.astype(jnp.int32) for there, _ in sides)
    pl.semaphore_wait(barrier, there_count)

    def copies(stage):
        base = stage * span
        face = GHOST * rows
        made = []
        for direction, (src, src_at, dst, dst_at, count) in enumerate((
            (field, base + pad, field, base + pad + cells, pad),
            (field, base + cells, field, base, pad),
            (yface, (stage * 2) * face, yhalo, (stage * 2 + 1) * face, face),
            (yface, (stage * 2 + 1) * face, yhalo, (stage * 2) * face, face),
        )):
            made.append(pltpu.make_async_remote_copy(
                src_ref=src.at[pl.ds(src_at, count)],
                dst_ref=dst.at[pl.ds(dst_at, count)],
                send_sem=send_sem.at[stage * 4 + direction],
                recv_sem=recv_sem.at[stage * 4 + direction],
                device_id=sides[direction][1],
                device_id_type=MESH,
            ))
        return made

    def one_stage(stage, carry):
        base = stage * span
        own = base + pad
        face = GHOST * rows
        sends = copies(stage)
        for direction in (0, 1):
            @pl.when(sides[direction][0])
            def _(direction=direction):
                sends[direction].start()
        for side in range(2):
            for n in range(GHOST):
                y = n if side == 0 else cols - GHOST + n
                for x in range(0, rows, 8):
                    yface[pl.ds((stage * 2 + side) * face + n * rows + x, 8)] = field[
                        pl.ds(own + x * cols + y, 8, stride=cols)
                    ]
        for direction in (2, 3):
            @pl.when(sides[direction][0])
            def _(direction=direction):
                sends[direction].start()

        def flip(block, carry):
            zin[pl.ds(pl.multiple_of(block * PITCH + ZPAD, 8), 128)] = field[
                pl.ds(pl.multiple_of(own + block * 128, 64), 128)
            ].T
            return carry

        lax.fori_loop(0, blocks, flip, 0, unroll=4)

        def z_cell(group, z):
            return zin[pl.ds(group * 8 * PITCH + ZPAD + z, 8, stride=PITCH)]

        depth = 128
        per = 4
        state = tuple(begin([z_cell(q, z) for z in range(-3, 2)]) for q in range(groups))
        firsts = [push(state[q], z_cell(q, 2)) for q in range(groups)]

        def z_steps(index, carry):
            start = index * per
            out = []
            for q in range(groups):
                st, behind = carry[q]
                for u in range(per):
                    z = start + u
                    st, next_behind, ahead = push(st, z_cell(q, z + 3))
                    at = pl.ds(q * 8 * OUT_PITCH + z, 8, stride=OUT_PITCH)
                    zout[at] = upwind(zsign[at], behind, ahead)
                    behind = next_behind
                out.append((st, behind))
            return tuple(out)

        lax.fori_loop(0, depth // per, z_steps, tuple((s, m) for s, m, _ in firsts))

        def unflip(block, carry):
            acc_z[pl.ds(pl.multiple_of(block * 128, 128), 128)] = zout[
                pl.ds(pl.multiple_of(block * OUT_PITCH, 8), 128)
            ].T
            return carry

        lax.fori_loop(0, blocks, unflip, 0, unroll=4)

        for direction, there in ((2, high_y), (3, low_y)):
            @pl.when(there)
            def _(direction=direction):
                sends[direction].wait_recv()

        ways = 2

        def y_block(pair, carry):
            xs = [(pair * ways + q) * 8 for q in range(ways)]

            def low_cell(x, n):
                return yhalo[pl.ds(pl.multiple_of((stage * 2) * face + n * rows + x, 8), 8)]

            def high_cell(x, n):
                return yhalo[pl.ds(pl.multiple_of((stage * 2 + 1) * face + n * rows + x, 8), 8)]

            def cell(x, y):
                return field[pl.ds(own + x * cols + y, 8, stride=cols)]

            def steps(start, count, carry, source):
                out = []
                for q, x in enumerate(xs):
                    st, behind = carry[q]
                    for u in range(count):
                        st, next_behind, ahead = push(st, source(x, u))
                        at = pl.ds(x * cols + start + u, 8, stride=cols)
                        acc_y[at] = upwind(sign[at], behind, ahead)
                        behind = next_behind
                    out.append((st, behind))
                return tuple(out)

            firsts = []
            for x in xs:
                st = begin([low_cell(x, n) for n in range(GHOST)] + [cell(x, 0), cell(x, 1)])
                st, behind, _ = push(st, cell(x, 2))
                firsts.append((st, behind))
            per = 4
            trips = (cols - GHOST) // per
            carry = lax.fori_loop(
                0, trips,
                lambda i, c: steps(i * per, per, c, lambda x, u: cell(x, i * per + u + GHOST)),
                tuple(firsts),
            )
            done = trips * per
            rest = cols - GHOST - done
            if rest:
                carry = steps(done, rest, carry, lambda x, u: cell(x, done + u + GHOST))
            steps(cols - GHOST, GHOST, carry, high_cell)
            return 0

        lax.fori_loop(0, rows // (8 * ways), y_block, 0)

        for direction, there in ((0, high_x), (1, low_x)):
            @pl.when(there)
            def _(direction=direction):
                sends[direction].wait_recv()

        odd = lax.rem(stage, 2) == 1
        last = jnp.where(stage == STAGES - 1, jnp.float32(1.0 / SCALE), jnp.float32(1.0))
        keep = jnp.where(odd, jnp.float32(0.5), jnp.float32(0.0)) * last
        take = jnp.where(odd, jnp.float32(0.5), jnp.float32(1.0)) * last
        before = jnp.maximum(stage - 1, 0) * span + pad
        after = base + span + pad

        def x_block(pair, carry):
            ys = [(pair * ways + q) * 8 for q in range(ways)]

            def cell(y, x):
                return field[pl.ds(pl.multiple_of(own + x * cols + y, 8), 8)]

            firsts = []
            for y in ys:
                st = begin([cell(y, x) for x in range(-3, 2)])
                st, behind, _ = push(st, cell(y, 2))
                firsts.append((st, behind))
            per = 4

            def steps(index, carry):
                out = []
                for q, y in enumerate(ys):
                    st, behind = carry[q]
                    for u in range(per):
                        x = index * per + u
                        st, next_behind, ahead = push(st, cell(y, x + 3))
                        off = pl.multiple_of(x * cols + y, 8)
                        at = pl.ds(off, 8)
                        total = upwind(sign[at], behind, ahead) + (acc_y[at] + acc_z[at])
                        moved = cell(y, x) - (speed[at] * STEP) * root(total)
                        older = field[pl.ds(pl.multiple_of(before + off, 8), 8)]
                        field[pl.ds(pl.multiple_of(after + off, 8), 8)] = keep * older + take * moved
                        behind = next_behind
                    out.append((st, behind))
                return tuple(out)

            lax.fori_loop(0, rows // per, steps, tuple(firsts))
            return 0

        lax.fori_loop(0, cols // (8 * ways), x_block, 0)

        for direction in range(4):
            @pl.when(sides[direction][0])
            def _(direction=direction):
                sends[direction].wait_send()
        return carry

    lax.fori_loop(0, STAGES, one_stage, 0)
    store = pltpu.make_async_copy(
        field.at[pl.ds(STAGES * span + pad, cells)], out_ref, local_sem.at[0]
    )
    store.start()
    store.wait()


def advance(level_set, normal_speed, rows, cols, n_gx, n_gy):
    cells = rows * cols
    blocks = cells // 128
    span = cells + 2 * GHOST * cols
    flat = pltpu.VMEM((cells, 128), jnp.float32)
    return pl.pallas_call(
        functools.partial(advance_kernel, rows, cols, n_gx, n_gy),
        out_shape=jax.ShapeDtypeStruct((cells, 128), jnp.float32),
        in_specs=[pl.BlockSpec(memory_space=pl.ANY)] * 2,
        out_specs=pl.BlockSpec(memory_space=pl.ANY),
        scratch_shapes=[
            pltpu.VMEM(((STAGES + 1) * span, 128), jnp.float32),
            flat, flat, flat, flat,
            pltpu.VMEM((blocks * PITCH, 128), jnp.float32),
            pltpu.VMEM((blocks * OUT_PITCH, 128), jnp.float32),
            pltpu.VMEM((blocks * OUT_PITCH, 128), jnp.float32),
            pltpu.VMEM((STAGES * 2 * GHOST * rows, 128), jnp.float32),
            pltpu.VMEM((STAGES * 2 * GHOST * rows, 128), jnp.float32),
            pltpu.SemaphoreType.DMA((STAGES * 4,)),
            pltpu.SemaphoreType.DMA((STAGES * 4,)),
            pltpu.SemaphoreType.DMA((2,)),
        ],
        compiler_params=pltpu.CompilerParams(
            collective_id=0, has_side_effects=True, vmem_limit_bytes=28 * 2**20
        ),
        name="advance",
    )(level_set, normal_speed)


def reinit_kernel(rows, cols, field, band, out, t, gain, sign):
    wide = cols // TILE
    down = rows // TILE

    def source(i, j, d):
        return pl.ds((d * TILE + i) * cols + j, wide, stride=TILE)

    def gather(i, carry):
        for j in range(TILE):
            v = jnp.concatenate([field[source(i, j, d)] for d in range(down)], axis=0)
            at = pl.ds(pl.multiple_of((i * TILE + j) * 8, 8), 8)
            t[0, at] = v
            gain[at] = (0.3 * v) * lax.rsqrt(v * v + 1.0)
            sign[at] = jnp.where(v > 0.0, 1.0, -1.0)
        return carry

    lax.fori_loop(0, TILE, gather, 0)
    lane = lax.broadcasted_iota(jnp.int32, (8, 128), 1)
    first = lane == 0

    def sweep(index, carry):
        now = lax.rem(index, 2)
        later = 1 - now

        def line(i, carry):
            above = jnp.maximum(i - 1, 0) * TILE
            below = jnp.minimum(i + 1, TILE - 1) * TILE
            here = i * TILE

            def cell(row, j):
                return t[now, pl.ds(pl.multiple_of((row + j) * 8, 8), 8)]

            values = [cell(here, j) for j in range(TILE)]
            for j in range(TILE):
                v = values[j]
                at = pl.ds(pl.multiple_of((here + j) * 8, 8), 8)
                s = sign[at]
                total = None
                mz = jnp.where(first, 0.0, v - pltpu.roll(v, 1, 1))
                pairs = [
                    (v - cell(above, j), v - cell(below, j)),
                    (v - values[max(j - 1, 0)], v - values[min(j + 1, TILE - 1)]),
                    (mz, -pltpu.roll(mz, 127, 1)),
                ]
                for m, nq in pairs:
                    u = jnp.maximum(jnp.maximum(s * m, s * nq), 0.0)
                    total = u * u if total is None else total + u * u
                t[later, at] = v - gain[at] * (root(total) - 1.0)
            return carry

        lax.fori_loop(0, TILE, line, 0)
        return carry

    lax.fori_loop(0, REINIT, sweep, 0)
    final = REINIT % 2

    def scatter(i, carry):
        for j in range(TILE):
            v = t[final, pl.ds(pl.multiple_of((i * TILE + j) * 8, 8), 8)]
            for d in range(down):
                at = source(i, j, d)
                mask = band[pl.ds(d * wide, wide)]
                out[at] = jnp.where(mask > 0, v[d * wide : (d + 1) * wide], field[at])
        return carry

    lax.fori_loop(0, TILE, scatter, 0)


def reinitialize(field, band, rows, cols):
    cells = rows * cols
    flat = pltpu.VMEM((cells, 128), jnp.float32)
    return pl.pallas_call(
        functools.partial(reinit_kernel, rows, cols),
        out_shape=jax.ShapeDtypeStruct((cells, 128), jnp.float32),
        in_specs=[pl.BlockSpec(memory_space=pltpu.VMEM)] * 2,
        out_specs=pl.BlockSpec(memory_space=pltpu.VMEM),
        scratch_shapes=[pltpu.VMEM((2, cells, 128), jnp.float32), flat, flat],
        compiler_params=pltpu.CompilerParams(vmem_limit_bytes=24 * 2**20),
        name="reinitialize",
    )(field, band)


def solution(mesh):
    n_gx, n_gy = mesh.shape["gx"], mesh.shape["gy"]

    def body(level_set, normal_speed, band_tiles):
        rows, cols, depth = level_set.shape
        cells = rows * cols
        field = advance(
            level_set.reshape(cells, depth), normal_speed.reshape(cells, depth),
            rows, cols, n_gx, n_gy,
        )
        band = jnp.broadcast_to(band_tiles.reshape(-1, 1), (band_tiles.size, 128))
        return reinitialize(field, band, rows, cols).reshape(rows, cols, depth)

    return jax.shard_map(
        body,
        mesh=mesh,
        in_specs=(
            P(("groups", "gx"), "gy", None),
            P(("groups", "gx"), "gy", None),
            P(("groups", "gx"), "gy"),
        ),
        out_specs=P(("groups", "gx"), "gy", None),
        check_vma=False,
    )
```

time: 176 us -> 180 us (1.023); the launches traced: 174 us -> 180 us
  Pallas kernels: 0 us -> 177 us
  other arithmetic: 102 us -> 0 us
  starting transfers between devices: 42.5 us -> 0 us
  waiting for transfers between devices: 17.4 us -> 0 us
  local copies, waits for them, and re-layouts: 11.5 us -> 3.28 us
    pallas_call x0 -> x2, Pallas kernels: none -> 177 us  [the longest x1 97.1 us: reinitialize(): pl.pallas_call(functools.partial(reinit_kernel, rows, cols), out_shape=ja...]
    sub x26 -> x0, other arithmetic: 68.9 us -> none  [the longest x12 31.9 us: one_sweep(): return current - REINIT_STEP * signum * (magnitude - 1.0)]
    ppermute x16 -> x0, starting transfers between devices: 42.5 us -> none  [the longest x8 32.1 us: extended(): lax.ppermute(lax.slice_in_dim(block, block.shape[dim] - width, None, axis...]
    add x2 -> x0, other arithmetic: 31.8 us -> none  [body(): 0.5 * surface + 0.5 * (halfway - TIME_STEP * section_rate(halfway))]
    ppermute x16 -> x0, waiting for transfers between devices: 17.4 us -> none  [the longest x8 10.4 us: extended(): lax.ppermute(lax.slice_in_dim(block, block.shape[dim] - width, None, axis...]
    slice x41 -> x0, local copies, waits for them, and re-layouts: 6.54 us -> none  [the longest x36 5.51 us: one_sweep(): padded = jnp.pad(current, widths, mode='edge')]
  transfers between devices with their start and end apart: 16 -> 0, of which waited for: 12 -> 0; matrix products, arithmetic and copies ran while one was open for 1% -> 0% of each run, Pallas kernels for 0% -> 0%
where the time goes in v1:
time: 180 us
  Pallas kernels  177 us (98%)
  local copies, waits for them, and re-layouts  3.28 us (2%)
    pallas_call x1, Pallas kernels, reinitialize(): pl.pallas_call(functools.partial(reinit_kernel, rows, cols), out_shape=ja...  97.1 us
    pallas_call x1, Pallas kernels, advance(): pl.pallas_call(functools.partial(advance_kernel, rows, cols, n_gx, n_gy),...  79.9 us

profile of v1, /device:TPU:0, one launch (start us, length us, event | category | flops | bytes accessed | tf_op | source)
XLA Modules:
  0.0 180.3 jit_solution(15762592940978388416)
XLA Ops:
  0.0 0.0 copy-start.2
  0.0 0.7 copy-done.2
  0.7 0.1 broadcast_in_dim.7
  0.8 0.1 broadcast_in_dim.8.band
  0.8 0.0 copy-start
  0.8 1.2 copy-done
  2.1 0.0 copy-start.1
  2.1 1.2 copy-done.1
  3.3 79.9 %advance.1.field = f32[2048,128]{1,0:T(8,128)S(1)} custom-call(f32[2048,128]{1,0:T(8,128)S(1)} %bitcast.3, f32[2048,128]{1,0:T(8,128)S(1)} %bitcast.4), custom_call_target="tpu_custom_call" | custom-call | tf_op jit(solution)/shard_map/advance/pallas_call | solution.py:358
  83.2 97.1 %reinitialize.1 = f32[2048,128]{1,0:T(8,128)} custom-call(f32[2048,128]{1,0:T(8,128)S(1)} %advance.1.field, s32[8,128]{1,0:T(8,128)S(1)} %broadcast_in_dim.8.band), custom_call_target="tpu_custom_call" | custom-call | tf_op jit(solution)/shard_map/reinitialize/pallas_call | solution.py:453
Async XLA Ops:
  0.0 0.7 copy-start.2
  0.8 1.2 copy-start
  2.1 1.2 copy-start.1

commit v2 on v1

v2 whole, which is shorter than its diff:
```python
import functools

import jax
import jax.numpy as jnp
from jax import lax
from jax.experimental import pallas as pl
from jax.experimental.pallas import tpu as pltpu
from jax.sharding import PartitionSpec as P

TILE = 16
RK_STEPS = 2
REINIT = 12
STAGES = 2 * RK_STEPS
GHOST = 3
SCALE = 1.5 ** 0.5
STEP = 0.125
EPS = 0.75e-6
TINY = 1e-37
PITCH = 140
OUT_PITCH = 132
ZPAD = 4
GAP = 8
UNROLL = 16
PARTS = 4
MESH = pl.DeviceIdType.MESH


def rcp(x):
    return pl.reciprocal(x, approx=True)


def root(x):
    return x * lax.rsqrt(jnp.maximum(x, TINY))


def stencil(x, y):
    e = y - x
    f = e * (1.0 / 3.0)
    mid = (e * f) * 2.0 + ((x * y) * 0.5 + EPS)
    left = mid + y * e
    right = mid - x * e
    rm = rcp(mid)
    rl = rcp(left)
    rr = rcp(right)
    b = (rm * rm) * 6.0
    a = rl * rl
    w = rr * rr
    a3 = a * 3.0
    w3 = w * 3.0
    r1 = y + f
    l1 = x - f
    return (
        (a, a3, a * (r1 + f), a3 * r1),
        (b, b * (y - f), b * (x + f)),
        (w, w3, w * (l1 - f), w3 * l1),
    )


def push(state, phi):
    last_phi, last_d, older_d, last_g, left_old, left_new, mid_new = state
    d = phi - last_phi
    g = d - last_d
    left, mid, right = stencil(last_g, g)
    a, a3, ar2, ar1 = left_old
    b, bc2, bc1 = mid_new
    w, w3, wl2, wl1 = right
    c2 = older_d + older_d
    behind = c2 + (ar2 + bc2 + wl1) * rcp(a + b + w3)
    ahead = (wl2 + bc1 + ar1) * rcp(w + b + a3) - c2
    return (phi, d, last_d, g, left_new, left, mid), behind, ahead


def begin(cells):
    p0, p1, p2, p3, p4 = cells
    d1, d2, d3, d4 = p1 - p0, p2 - p1, p3 - p2, p4 - p3
    g1, g2, g3 = d2 - d1, d3 - d2, d4 - d3
    left_a, _, _ = stencil(g1, g2)
    left_b, mid_b, _ = stencil(g2, g3)
    return (p4, d4, d3, g3, left_a, left_b, mid_b)


def upwind(sign, behind, ahead):
    v = jnp.maximum(jnp.maximum(sign * behind, sign * ahead), 0.0)
    return v * v


def advance_kernel(
    rows, cols, n_gx, n_gy,
    level_hbm, speed_hbm, out_ref,
    field_a, field_b, speed, sign, acc_y, acc_z, zin, zout, zsign, yface, yhalo,
    send_sem, recv_sem, local_sem, store_sem,
):
    cells = rows * cols
    pitch = cols + GAP
    own = GHOST * pitch
    blocks = cells // 128
    block_rows = 128 // cols
    groups = blocks // 8
    face = GHOST * rows
    gx = lax.axis_index("gx")
    gy = lax.axis_index("gy")
    low_x, high_x = gx > 0, gx < n_gx - 1
    low_y, high_y = gy > 0, gy < n_gy - 1
    sides = (
        (low_x, {"gx": gx - 1}), (high_x, {"gx": gx + 1}),
        (low_y, {"gy": gy - 1}), (high_y, {"gy": gy + 1}),
    )

    part = cells // PARTS
    loads = []
    for n in range(PARTS):
        at = pl.ds(n * part, part)
        loads.append((
            pltpu.make_async_copy(level_hbm.at[at], acc_z.at[at], local_sem.at[n]),
            pltpu.make_async_copy(speed_hbm.at[at], speed.at[at], local_sem.at[PARTS + n]),
        ))
    for level, _ in loads:
        level.start()
    for _, rate in loads:
        rate.start()

    barrier = pltpu.get_barrier_semaphore()
    for there, device in sides:
        @pl.when(there)
        def _():
            pl.semaphore_signal(barrier, inc=1, device_id=device, device_id_type=MESH)

    zero = jnp.zeros((own, 128), jnp.float32)
    gap = jnp.zeros((GAP, 128), jnp.float32)
    for field in (field_a, field_b):
        for x in range(rows):
            field[pl.ds(own + x * pitch + cols, GAP)] = gap

        @pl.when(jnp.logical_not(low_x))
        def _():
            field[pl.ds(0, own)] = zero

        @pl.when(jnp.logical_not(high_x))
        def _():
            field[pl.ds(own + rows * pitch, own)] = zero

    for stage in range(STAGES):
        @pl.when(jnp.logical_not(low_y))
        def _():
            yhalo[pl.ds((stage * 2) * face, face)] = zero[:face]

        @pl.when(jnp.logical_not(high_y))
        def _():
            yhalo[pl.ds((stage * 2 + 1) * face, face)] = zero[:face]

    for block in range(blocks):
        zin[pl.ds(block * PITCH, ZPAD)] = gap[:ZPAD]
        zin[pl.ds(block * PITCH + ZPAD + 128, PITCH - 128 - ZPAD)] = gap[: PITCH - 128 - ZPAD]

    def natural(x, y):
        return pl.ds(pl.multiple_of(x * cols + y, 8), 8)

    def spaced(x, y):
        return pl.ds(pl.multiple_of(x * pitch + y, 8), 8)

    for level, _ in loads:
        level.wait()

    def scaled(x, carry):
        field_a[pl.ds(pl.multiple_of(own + x * pitch, 8), cols)] = (
            acc_z[pl.ds(pl.multiple_of(x * cols, 8), cols)] * SCALE
        )
        return carry

    lax.fori_loop(0, rows, scaled, 0)
    for _, rate in loads:
        rate.wait()

    def signs(block, carry):
        v = jnp.where(speed[pl.ds(pl.multiple_of(block * 128, 128), 128)] > 0.0, 1.0, -1.0)
        for n in range(block_rows):
            at = pl.ds(pl.multiple_of((block * block_rows + n) * pitch, 8), cols)
            sign[at] = v[n * cols : (n + 1) * cols]
        zsign[pl.ds(block * OUT_PITCH, 128)] = v.T
        return carry

    lax.fori_loop(0, blocks, signs, 0)

    there_count = sum(there.astype(jnp.int32) for there, _ in sides)
    pl.semaphore_wait(barrier, there_count)

    def one_stage(stage, field, fresh, finish):
        sends = []
        for direction, (src, src_at, dst, dst_at, count) in enumerate((
            (field, own, field, own + rows * pitch, own),
            (field, rows * pitch, field, 0, own),
            (yface, (stage * 2) * face, yhalo, (stage * 2 + 1) * face, face),
            (yface, (stage * 2 + 1) * face, yhalo, (stage * 2) * face, face),
        )):
            sends.append(pltpu.make_async_remote_copy(
                src_ref=src.at[pl.ds(src_at, count)],
                dst_ref=dst.at[pl.ds(dst_at, count)],
                send_sem=send_sem.at[stage * 4 + direction],
                recv_sem=recv_sem.at[stage * 4 + direction],
                device_id=sides[direction][1],
                device_id_type=MESH,
            ))
        for direction in (0, 1):
            @pl.when(sides[direction][0])
            def _(direction=direction):
                sends[direction].start()
        for side in range(2):
            for n in range(GHOST):
                y = n if side == 0 else cols - GHOST + n
                for x in range(0, rows, 8):
                    yface[pl.ds((stage * 2 + side) * face + n * rows + x, 8)] = field[
                        pl.ds(own + x * pitch + y, 8, stride=pitch)
                    ]
        for direction in (2, 3):
            @pl.when(sides[direction][0])
            def _(direction=direction):
                sends[direction].start()

        def flip(block, carry):
            v = [
                field[pl.ds(pl.multiple_of(own + (block * block_rows + n) * pitch, 8), cols)]
                for n in range(block_rows)
            ]
            zin[pl.ds(block * PITCH + ZPAD, 128)] = jnp.concatenate(v, axis=0).T
            return carry

        lax.fori_loop(0, blocks, flip, 0, unroll=True)

        def z_cell(group, z):
            return zin[pl.ds(group * 8 * PITCH + ZPAD + z, 8, stride=PITCH)]

        depth = 128

        def z_group(q, carry):
            state = begin([z_cell(q, z) for z in range(-3, 2)])
            first = push(state, z_cell(q, 2))

            def z_steps(index, carry):
                st, behind = carry
                for u in range(UNROLL):
                    z = index * UNROLL + u
                    st, next_behind, ahead = push(st, z_cell(q, z + 3))
                    at = pl.ds(q * 8 * OUT_PITCH + z, 8, stride=OUT_PITCH)
                    zout[at] = upwind(zsign[at], behind, ahead)
                    behind = next_behind
                return st, behind

            lax.fori_loop(0, depth // UNROLL, z_steps, first[:2])
            return carry

        lax.fori_loop(0, groups, z_group, 0)

        def unflip(block, carry):
            acc_z[pl.ds(pl.multiple_of(block * 128, 128), 128)] = zout[
                pl.ds(block * OUT_PITCH, 128)
            ].T
            return carry

        lax.fori_loop(0, blocks, unflip, 0, unroll=True)

        for direction, there in ((2, high_y), (3, low_y)):
            @pl.when(there)
            def _(direction=direction):
                sends[direction].wait_recv()

        def y_block(block, carry):
            x = block * 8

            def low_cell(n):
                return yhalo[pl.ds(pl.multiple_of((stage * 2) * face + n * rows + x, 8), 8)]

            def high_cell(n):
                return yhalo[pl.ds(pl.multiple_of((stage * 2 + 1) * face + n * rows + x, 8), 8)]

            def cell(y):
                return field[pl.ds(own + x * pitch + y, 8, stride=pitch)]

            def steps(start, count, carry, source):
                st, behind = carry
                for u in range(count):
                    st, next_behind, ahead = push(st, source(u))
                    at = pl.ds(x * pitch + start + u, 8, stride=pitch)
                    acc_y[at] = upwind(sign[at], behind, ahead)
                    behind = next_behind
                return st, behind

            st = begin([low_cell(n) for n in range(GHOST)] + [cell(0), cell(1)])
            carried = push(st, cell(2))[:2]
            trips = (cols - GHOST) // UNROLL
            carried = lax.fori_loop(
                0, trips,
                lambda i, c: steps(i * UNROLL, UNROLL, c, lambda u: cell(i * UNROLL + u + GHOST)),
                carried,
            )
            done = trips * UNROLL
            rest = cols - GHOST - done
            steps(done, rest + GHOST, carried, lambda u: (
                cell(done + u + GHOST) if u < rest else high_cell(u - rest)
            ))
            return carry

        lax.fori_loop(0, rows // 8, y_block, 0)

        for direction, there in ((0, high_x), (1, low_x)):
            @pl.when(there)
            def _(direction=direction):
                sends[direction].wait_recv()

        def x_block(block, carry):
            y = block * 8

            def cell(x):
                return field[spaced(x + GHOST, y)]

            st = begin([cell(x) for x in range(-3, 2)])
            carried = push(st, cell(2))[:2]

            def steps(index, carry):
                st, behind = carry
                for u in range(UNROLL):
                    x = index * UNROLL + u
                    st, next_behind, ahead = push(st, cell(x + 3))
                    at, here = spaced(x, y), natural(x, y)
                    total = upwind(sign[at], behind, ahead) + (acc_y[at] + acc_z[here])
                    moved = cell(x) - (speed[here] * STEP) * root(total)
                    fresh[spaced(x + GHOST, y)] = finish(moved, spaced(x + GHOST, y))
                    behind = next_behind
                return st, behind

            lax.fori_loop(0, rows // UNROLL, steps, carried)
            return carry

        lax.fori_loop(0, cols // 8, x_block, 0)

        for direction in range(4):
            @pl.when(sides[direction][0])
            def _(direction=direction):
                sends[direction].wait_send()

    def time_step(step, carry):
        last = jnp.where(step == RK_STEPS - 1, jnp.float32(0.5 / SCALE), jnp.float32(0.5))
        one_stage(2 * step, field_a, field_b, lambda moved, at: moved)
        one_stage(2 * step + 1, field_b, field_a, lambda moved, at: last * (field_a[at] + moved))
        return carry

    lax.fori_loop(0, RK_STEPS, time_step, 0)
    stores = []
    for x in range(rows):
        stores.append(pltpu.make_async_copy(
            field_a.at[pl.ds(own + x * pitch, cols)], out_ref.at[pl.ds(x * cols, cols)],
            store_sem.at[x],
        ))
        stores[-1].start()
    for store in stores:
        store.wait()


def advance(level_set, normal_speed, rows, cols, n_gx, n_gy):
    cells = rows * cols
    blocks = cells // 128
    pitch = cols + GAP
    flat = pltpu.VMEM((cells, 128), jnp.float32)
    spaced = pltpu.VMEM((rows * pitch, 128), jnp.float32)
    padded = pltpu.VMEM(((rows + 2 * GHOST) * pitch, 128), jnp.float32)
    return pl.pallas_call(
        functools.partial(advance_kernel, rows, cols, n_gx, n_gy),
        out_shape=jax.ShapeDtypeStruct((cells, 128), jnp.float32),
        in_specs=[pl.BlockSpec(memory_space=pltpu.HBM)] * 2,
        out_specs=pl.BlockSpec(memory_space=pl.ANY),
        scratch_shapes=[
            padded, padded, flat, spaced, spaced, flat,
            pltpu.VMEM((blocks * PITCH, 128), jnp.float32),
            pltpu.VMEM((blocks * OUT_PITCH, 128), jnp.float32),
            pltpu.VMEM((blocks * OUT_PITCH, 128), jnp.float32),
            pltpu.VMEM((STAGES * 2 * GHOST * rows, 128), jnp.float32),
            pltpu.VMEM((STAGES * 2 * GHOST * rows, 128), jnp.float32),
            pltpu.SemaphoreType.DMA((STAGES * 4,)),
            pltpu.SemaphoreType.DMA((STAGES * 4,)),
            pltpu.SemaphoreType.DMA((2 * PARTS,)),
            pltpu.SemaphoreType.DMA((rows,)),
        ],
        compiler_params=pltpu.CompilerParams(
            collective_id=0, has_side_effects=True, vmem_limit_bytes=28 * 2**20
        ),
        name="advance",
    )(level_set, normal_speed)


def reinit_kernel(rows, cols, field, band, out, t_a, t_b, gain, sign):
    wide = cols // TILE
    down = rows // TILE

    def source(i, j, d):
        return pl.ds((d * TILE + i) * cols + j, wide, stride=TILE)

    def gather(i, carry):
        for j in range(TILE):
            v = jnp.concatenate([field[source(i, j, d)] for d in range(down)], axis=0)
            at = pl.ds(pl.multiple_of((i * TILE + j) * 8, 8), 8)
            t_a[at] = v
            gain[at] = (0.3 * v) * lax.rsqrt(v * v + 1.0)
            sign[at] = jnp.where(v > 0.0, 1.0, -1.0)
        return carry

    lax.fori_loop(0, TILE, gather, 0)
    lane = lax.broadcasted_iota(jnp.int32, (8, 128), 1)
    first = lane == 0

    def sweep(now, later):
        def line(i, carry):
            above = jnp.maximum(i - 1, 0) * TILE
            below = jnp.minimum(i + 1, TILE - 1) * TILE
            here = i * TILE

            def cell(row, j):
                return now[pl.ds(pl.multiple_of((row + j) * 8, 8), 8)]

            values = [cell(here, j) for j in range(TILE)]
            for j in range(TILE):
                v = values[j]
                at = pl.ds(pl.multiple_of((here + j) * 8, 8), 8)
                s = sign[at]
                total = None
                mz = jnp.where(first, 0.0, v - pltpu.roll(v, 1, 1))
                pairs = [
                    (v - cell(above, j), v - cell(below, j)),
                    (v - values[max(j - 1, 0)], v - values[min(j + 1, TILE - 1)]),
                    (mz, -pltpu.roll(mz, 127, 1)),
                ]
                for m, nq in pairs:
                    u = jnp.maximum(jnp.maximum(s * m, s * nq), 0.0)
                    total = u * u if total is None else total + u * u
                later[at] = v - gain[at] * (root(total) - 1.0)
            return carry

        lax.fori_loop(0, TILE, line, 0)

    def sweeps(index, carry):
        sweep(t_a, t_b)
        sweep(t_b, t_a)
        return carry

    lax.fori_loop(0, REINIT // 2, sweeps, 0)

    def scatter(i, carry):
        for j in range(TILE):
            v = t_a[pl.ds(pl.multiple_of((i * TILE + j) * 8, 8), 8)]
            for d in range(down):
                at = source(i, j, d)
                mask = band[pl.ds(d * wide, wide)]
                out[at] = jnp.where(mask > 0, v[d * wide : (d + 1) * wide], field[at])
        return carry

    lax.fori_loop(0, TILE, scatter, 0)


def reinitialize(field, band, rows, cols):
    cells = rows * cols
    flat = pltpu.VMEM((cells, 128), jnp.float32)
    return pl.pallas_call(
        functools.partial(reinit_kernel, rows, cols),
        out_shape=jax.ShapeDtypeStruct((cells, 128), jnp.float32),
        in_specs=[pl.BlockSpec(memory_space=pltpu.VMEM)] * 2,
        out_specs=pl.BlockSpec(memory_space=pltpu.VMEM),
        scratch_shapes=[flat, flat, flat, flat],
        compiler_params=pltpu.CompilerParams(vmem_limit_bytes=24 * 2**20),
        name="reinitialize",
    )(field, band)


def solution(mesh):
    n_gx, n_gy = mesh.shape["gx"], mesh.shape["gy"]

    def body(level_set, normal_speed, band_tiles):
        rows, cols, depth = level_set.shape
        cells = rows * cols
        field = advance(
            level_set.reshape(cells, depth), normal_speed.reshape(cells, depth),
            rows, cols, n_gx, n_gy,
        )
        band = jnp.broadcast_to(band_tiles.reshape(-1, 1), (band_tiles.size, 128))
        return reinitialize(field, band, rows, cols).reshape(rows, cols, depth)

    return jax.shard_map(
        body,
        mesh=mesh,
        in_specs=(
            P(("groups", "gx"), "gy", None),
            P(("groups", "gx"), "gy", None),
            P(("groups", "gx"), "gy"),
        ),
        out_specs=P(("groups", "gx"), "gy", None),
        check_vma=False,
    )
```

time: 180 us -> 80.7 us (0.45)
  the two profiles are of different devices: /device:TPU:0 before, /device:TPU:17 now
where the time goes in v2:
time: 80.7 us; the launch traced here: 80.5 us
  Pallas kernels  77.2 us (96%)
  local copies, waits for them, and re-layouts  3.28 us (4%)
    pallas_call x1, Pallas kernels, advance(): pl.pallas_call(functools.partial(advance_kernel, rows, cols, n_gx, n_gy),...  40.9 us
    pallas_call x1, Pallas kernels, reinitialize(): pl.pallas_call(functools.partial(reinit_kernel, rows, cols), out_shape=ja...  36.3 us
    unnamed x6, local copies, waits for them, and re-layouts  3.13 us

profile of v2, /device:TPU:17, one launch (start us, length us, event | category | flops | bytes accessed | tf_op | source)
XLA Modules:
  0.0 80.5 jit_solution(18231112724091852178)
XLA Ops:
  0.0 0.0 copy-start.2
  0.0 0.7 copy-done.2
  0.7 0.1 broadcast_in_dim.7
  0.8 0.1 broadcast_in_dim.8.band
  0.8 0.0 copy-start
  0.8 1.2 %copy-done = f32[32,64,128]{2,1,0:T(8,128)S(1)} copy-done((f32[32,64,128]{2,1,0:T(8,128)S(1)}, f32[32,64,128]{2,1,0:T(8,128)}, u32[]{:S(2)}) %copy-start) | copy-done | bytes 1048600
  2.1 0.0 copy-start.1
  2.1 1.2 %copy-done.1 = f32[32,64,128]{2,1,0:T(8,128)S(1)} copy-done((f32[32,64,128]{2,1,0:T(8,128)S(1)}, f32[32,64,128]{2,1,0:T(8,128)}, u32[]{:S(2)}) %copy-start.1) | copy-done | bytes 1048600
  3.3 40.9 %advance.1.field = f32[2048,128]{1,0:T(8,128)S(1)} custom-call(f32[2048,128]{1,0:T(8,128)S(1)} %bitcast.3, f32[2048,128]{1,0:T(8,128)S(1)} %bitcast.4), custom_call_target="tpu_custom_call" | custom-call | tf_op jit(solution)/shard_map/advance/pallas_call | solution.py:365
  44.1 36.3 %reinitialize.1 = f32[2048,128]{1,0:T(8,128)} custom-call(f32[2048,128]{1,0:T(8,128)S(1)} %advance.1.field, s32[8,128]{1,0:T(8,128)S(1)} %broadcast_in_dim.8.band), custom_call_target="tpu_custom_call" | custom-call | tf_op jit(solution)/shard_map/reinitialize/pallas_call | solution.py:460
Async XLA Ops:
  0.0 0.7 copy-start.2
  0.8 1.2 %copy-start = (f32[32,64,128]{2,1,0:T(8,128)S(1)}, f32[32,64,128]{2,1,0:T(8,128)}, u32[]{:S(2)}) copy-start(f32[32,64,128]{2,1,0:T(8,128)} %param.3) | copy-start | bytes 3145732
  2.1 1.2 %copy-start.1 = (f32[32,64,128]{2,1,0:T(8,128)S(1)}, f32[32,64,128]{2,1,0:T(8,128)}, u32[]{:S(2)}) copy-start(f32[32,64,128]{2,1,0:T(8,128)} %param.4) | copy-start | bytes 3145732

commit v3 on v2

v3 whole, which is shorter than its diff:
```python
import functools

import jax
import jax.numpy as jnp
from jax import lax
from jax.experimental import pallas as pl
from jax.experimental.pallas import tpu as pltpu
from jax.sharding import PartitionSpec as P

TILE = 16
RK_STEPS = 2
REINIT = 12
STAGES = 2 * RK_STEPS
GHOST = 3
SCALE = 1.5 ** 0.5
STEP = 0.125
EPS = 0.375e-6
TINY = 1e-37
FLOOR = 1e-18
PITCH = 140
OUT_PITCH = 132
ZPAD = 4
GAP = 8
Z_STEPS = 32
Y_TRIPS = 2
PARTS = 4
MESH = pl.DeviceIdType.MESH


def rcp(x):
    return pl.reciprocal(x, approx=True)


def root(x):
    return x * lax.rsqrt(jnp.maximum(x, TINY))


def stencil(e, f, half_x, half_y):
    mid = e * f + (half_x * half_y + EPS)
    rl = rcp(mid + half_y * e)
    rr = rcp(mid - half_x * e)
    rm = rcp(mid)
    return rl * rl, (rm * rm) * 6.0, rr * rr


def push(state, phi):
    last_phi, last_d, last_pair, older_pair, last_g, last_half, last_f, delta, a, left, b = state
    d = phi - last_phi
    g = d - last_d
    pair = d + last_d
    half = g * 0.5
    e = g - last_g
    f = e * (1.0 / 3.0)
    next_delta = last_f - f
    next_left, next_mid, w = stencil(e, f, last_half, half)
    aa = a * delta
    ww = w * next_delta
    both = aa + ww
    both = both + both
    weights = a + b + w
    behind = (last_pair - last_f) + (both + ww) * rcp(weights + (w + w))
    ahead = (both + aa) * rcp(weights + (a + a)) - (older_pair - last_f)
    state = (phi, d, pair, last_pair, g, half, f, next_delta, left, next_left, next_mid)
    return state, behind, ahead


def begin(cells):
    p0, p1, p2, p3, p4 = cells
    d1, d2, d3, d4 = p1 - p0, p2 - p1, p3 - p2, p4 - p3
    g1, g2, g3 = d2 - d1, d3 - d2, d4 - d3
    h1, h2, h3 = g1 * 0.5, g2 * 0.5, g3 * 0.5
    e1, e2 = g2 - g1, g3 - g2
    f1, f2 = e1 * (1.0 / 3.0), e2 * (1.0 / 3.0)
    left_a, _, _ = stencil(e1, f1, h1, h2)
    left_b, mid_b, _ = stencil(e2, f2, h2, h3)
    return (p4, d4, d4 + d3, d3 + d2, g3, h3, f2, f1 - f2, left_a, left_b, mid_b)


def upwind(sign, behind, ahead):
    v = jnp.maximum(jnp.maximum(sign * behind, sign * ahead), 0.0)
    return v * v


def advance_kernel(
    rows, cols, n_gx, n_gy,
    level_hbm, speed_hbm, out_ref,
    field_a, field_b, kept, speed, rate, sign, acc_y, acc_z, zin, zout, zsign, yface, yhalo,
    send_sem, recv_sem, local_sem,
):
    cells = rows * cols
    pitch = cols + GAP
    own = GHOST * pitch
    blocks = cells // 128
    block_rows = 128 // cols
    groups = blocks // 8
    face = GHOST * rows
    gx = lax.axis_index("gx")
    gy = lax.axis_index("gy")
    low_x, high_x = gx > 0, gx < n_gx - 1
    low_y, high_y = gy > 0, gy < n_gy - 1
    sides = (
        (low_x, {"gx": gx - 1}), (high_x, {"gx": gx + 1}),
        (low_y, {"gy": gy - 1}), (high_y, {"gy": gy + 1}),
    )

    part = cells // PARTS
    loads = []
    for n in range(PARTS):
        at = pl.ds(n * part, part)
        loads.append((
            pltpu.make_async_copy(level_hbm.at[at], acc_z.at[at], local_sem.at[n]),
            pltpu.make_async_copy(speed_hbm.at[at], speed.at[at], local_sem.at[PARTS + n]),
        ))
    for level, _ in loads:
        level.start()
    for _, moving in loads:
        moving.start()

    barrier = pltpu.get_barrier_semaphore()
    for there, device in sides:
        @pl.when(there)
        def _():
            pl.semaphore_signal(barrier, inc=1, device_id=device, device_id_type=MESH)

    zero = jnp.zeros((own, 128), jnp.float32)
    gap = jnp.zeros((GAP, 128), jnp.float32)
    for field in (field_a, field_b):
        for x in range(rows):
            field[pl.ds(own + x * pitch + cols, GAP)] = gap

        @pl.when(jnp.logical_not(low_x))
        def _():
            field[pl.ds(0, own)] = zero

        @pl.when(jnp.logical_not(high_x))
        def _():
            field[pl.ds(own + rows * pitch, own)] = zero

    for stage in range(STAGES):
        @pl.when(jnp.logical_not(low_y))
        def _():
            yhalo[pl.ds((stage * 2) * face, face)] = zero[:face]

        @pl.when(jnp.logical_not(high_y))
        def _():
            yhalo[pl.ds((stage * 2 + 1) * face, face)] = zero[:face]

    for q in range(groups):
        for block in range(8):
            at = block * PITCH
            zin[q][pl.ds(at, ZPAD)] = gap[:ZPAD]
            zin[q][pl.ds(at + ZPAD + 128, PITCH - 128 - ZPAD)] = gap[: PITCH - 128 - ZPAD]

    def natural(x, y):
        return pl.ds(pl.multiple_of(x * cols + y, 8), 8)

    def spaced(x, y):
        return pl.ds(pl.multiple_of(x * pitch + y, 8), 8)

    for level, _ in loads:
        level.wait()

    def scaled(x, carry):
        field_a[pl.ds(pl.multiple_of(own + x * pitch, 8), cols)] = (
            acc_z[pl.ds(pl.multiple_of(x * cols, 8), cols)] * SCALE
        )
        return carry

    lax.fori_loop(0, rows, scaled, 0, unroll=True)
    for _, moving in loads:
        moving.wait()

    def signs(block, carry):
        here = pl.ds(pl.multiple_of(block * 128, 128), 128)
        v = jnp.where(speed[here] > 0.0, 1.0, -1.0)
        rate[here] = speed[here] * STEP
        for n in range(block_rows):
            at = pl.ds(pl.multiple_of((block * block_rows + n) * pitch, 8), cols)
            sign[at] = v[n * cols : (n + 1) * cols]
        return v

    for q in range(groups):
        def sign_block(block, carry):
            v = signs(q * 8 + block, carry)
            zsign[q][pl.ds(block * OUT_PITCH, 128)] = v.T
            return carry

        lax.fori_loop(0, 8, sign_block, 0, unroll=True)

    there_count = sum(there.astype(jnp.int32) for there, _ in sides)
    pl.semaphore_wait(barrier, there_count)

    def one_stage(stage, field, write):
        sends = []
        for direction, (src, src_at, dst, dst_at, count) in enumerate((
            (field, own, field, own + rows * pitch, own),
            (field, rows * pitch, field, 0, own),
            (yface, (stage * 2) * face, yhalo, (stage * 2 + 1) * face, face),
            (yface, (stage * 2 + 1) * face, yhalo, (stage * 2) * face, face),
        )):
            sends.append(pltpu.make_async_remote_copy(
                src_ref=src.at[pl.ds(src_at, count)],
                dst_ref=dst.at[pl.ds(dst_at, count)],
                send_sem=send_sem.at[stage * 4 + direction],
                recv_sem=recv_sem.at[stage * 4 + direction],
                device_id=sides[direction][1],
                device_id_type=MESH,
            ))
        for direction in (0, 1):
            @pl.when(sides[direction][0])
            def _(direction=direction):
                sends[direction].start()
        for side in range(2):
            for n in range(GHOST):
                y = n if side == 0 else cols - GHOST + n
                for x in range(0, rows, 8):
                    yface[pl.ds((stage * 2 + side) * face + n * rows + x, 8)] = field[
                        pl.ds(own + x * pitch + y, 8, stride=pitch)
                    ]
        for direction in (2, 3):
            @pl.when(sides[direction][0])
            def _(direction=direction):
                sends[direction].start()

        def flip(q, block):
            v = []
            for n in range(block_rows):
                x = (q * 8 + block) * block_rows + n
                v.append(field[pl.ds(pl.multiple_of(own + x * pitch, 8), cols)])
            zin[q][pl.ds(block * PITCH + ZPAD, 128)] = jnp.concatenate(v, axis=0).T

        def unflip(q, block):
            acc_z[pl.ds(pl.multiple_of((q * 8 + block) * 128, 128), 128)] = zout[q][
                pl.ds(block * OUT_PITCH, 128)
            ].T

        def flip_first(block, carry):
            flip(0, block)
            return carry

        lax.fori_loop(0, 8, flip_first, 0, unroll=True)
        trips = 128 // Z_STEPS
        for q in range(groups):
            def z_cell(z):
                return zin[q][pl.ds(ZPAD + z, 8, stride=PITCH)]

            def z_trip(trip, carry):
                def step(u, carry):
                    st, behind = carry
                    z = trip * Z_STEPS + u
                    st, next_behind, ahead = push(st, z_cell(z + 3))
                    at = pl.ds(z, 8, stride=OUT_PITCH)
                    zout[q][at] = upwind(zsign[q][at], behind, ahead)
                    return st, next_behind

                for n in range(8 // trips):
                    if q + 1 < groups:
                        flip(q + 1, trip * (8 // trips) + n)
                    if q > 0:
                        unflip(q - 1, trip * (8 // trips) + n)
                return lax.fori_loop(0, Z_STEPS, step, carry, unroll=True)

            first = push(begin([z_cell(z) for z in range(-3, 2)]), z_cell(2))
            lax.fori_loop(0, trips, z_trip, first[:2])

        for direction, there in ((2, high_y), (3, low_y)):
            @pl.when(there)
            def _(direction=direction):
                sends[direction].wait_recv()

        def y_block(block, carry):
            x = block * 8

            def low_cell(n):
                return yhalo[pl.ds(pl.multiple_of((stage * 2) * face + n * rows + x, 8), 8)]

            def high_cell(n):
                return yhalo[pl.ds(pl.multiple_of((stage * 2 + 1) * face + n * rows + x, 8), 8)]

            def cell(y):
                return field[pl.ds(own + x * pitch + y, 8, stride=pitch)]

            def step(y, carry, phi):
                st, behind = carry
                st, next_behind, ahead = push(st, phi)
                at = pl.ds(x * pitch + y, 8, stride=pitch)
                acc_y[at] = upwind(sign[at], behind, ahead)
                return st, next_behind

            st = begin([low_cell(n) for n in range(GHOST)] + [cell(0), cell(1)])
            carried = push(st, cell(2))[:2]
            count = (cols - GHOST) // Y_TRIPS

            def y_trip(trip, carried):
                unflip(groups - 1, block * Y_TRIPS + trip)
                start = trip * count
                return lax.fori_loop(
                    0, count,
                    lambda u, c: step(start + u, c, cell(start + u + GHOST)),
                    carried, unroll=True,
                )

            carried = lax.fori_loop(0, Y_TRIPS, y_trip, carried)
            for y in range(count * Y_TRIPS, cols):
                ahead = y + GHOST
                phi = cell(ahead) if ahead < cols else high_cell(ahead - cols)
                carried = step(y, carried, phi)
            return carry

        lax.fori_loop(0, rows // 8, y_block, 0)

        for direction, there in ((0, high_x), (1, low_x)):
            @pl.when(there)
            def _(direction=direction):
                sends[direction].wait_recv()

        def x_block(block, carry):
            y = block * 8

            def cell(x):
                return field[spaced(x + GHOST, y)]

            st = begin([cell(x) for x in range(-3, 2)])
            carried = push(st, cell(2))[:2]

            def step(x, carry):
                st, behind = carry
                st, next_behind, ahead = push(st, cell(x + 3))
                at, here = spaced(x, y), natural(x, y)
                total = upwind(sign[at], behind, ahead) + (acc_y[at] + acc_z[here])
                now = cell(x)
                write(now, now - rate[here] * root(total), spaced(x + GHOST, y), here)
                return st, next_behind

            lax.fori_loop(0, rows, step, carried, unroll=True)
            return carry

        lax.fori_loop(0, cols // 8, x_block, 0)

        for direction in range(4):
            @pl.when(sides[direction][0])
            def _(direction=direction):
                sends[direction].wait_send()

    def time_step(step, carry):
        last = jnp.where(step == RK_STEPS - 1, jnp.float32(0.5 / SCALE), jnp.float32(0.5))

        def halfway(now, moved, at, here):
            field_b[at] = moved
            kept[here] = now

        def whole(now, moved, at, here):
            result = last * (kept[here] + moved)
            field_a[at] = result
            out_ref[here] = result

        one_stage(2 * step, field_a, halfway)
        one_stage(2 * step + 1, field_b, whole)
        return carry

    lax.fori_loop(0, RK_STEPS, time_step, 0)


def advance(level_set, normal_speed, rows, cols, n_gx, n_gy):
    cells = rows * cols
    groups = cells // 1024
    pitch = cols + GAP
    flat = pltpu.VMEM((cells, 128), jnp.float32)
    spaced = pltpu.VMEM((rows * pitch, 128), jnp.float32)
    padded = pltpu.VMEM(((rows + 2 * GHOST) * pitch, 128), jnp.float32)
    return pl.pallas_call(
        functools.partial(advance_kernel, rows, cols, n_gx, n_gy),
        out_shape=jax.ShapeDtypeStruct((cells, 128), jnp.float32),
        in_specs=[pl.BlockSpec(memory_space=pltpu.HBM)] * 2,
        out_specs=pl.BlockSpec(memory_space=pltpu.VMEM),
        scratch_shapes=[
            padded, padded, flat, flat, flat, spaced, spaced, flat,
            [pltpu.VMEM((8 * PITCH, 128), jnp.float32)] * groups,
            [pltpu.VMEM((8 * OUT_PITCH, 128), jnp.float32)] * groups,
            [pltpu.VMEM((8 * OUT_PITCH, 128), jnp.float32)] * groups,
            pltpu.VMEM((STAGES * 2 * GHOST * rows, 128), jnp.float32),
            pltpu.VMEM((STAGES * 2 * GHOST * rows, 128), jnp.float32),
            pltpu.SemaphoreType.DMA((STAGES * 4,)),
            pltpu.SemaphoreType.DMA((STAGES * 4,)),
            pltpu.SemaphoreType.DMA((2 * PARTS,)),
        ],
        compiler_params=pltpu.CompilerParams(
            collective_id=0, has_side_effects=True, vmem_limit_bytes=28 * 2**20
        ),
        name="advance",
    )(level_set, normal_speed)


def reinit_kernel(rows, cols, field, band, out, t_a, t_b, gain, sign, store_sem, merged):
    wide = cols // TILE
    down = rows // TILE
    lane = lax.broadcasted_iota(jnp.int32, (8, 128), 1)
    inner = jnp.where(lane == 0, 0.0, 1.0)
    slot = lax.broadcasted_iota(jnp.int32, (8, 128), 0)
    chosen = jnp.zeros((8, 128), jnp.int32)
    for d in range(down):
        for w in range(wide):
            chosen = jnp.where(slot == d * wide + w, band[d, w], chosen)

    def source(i, j, d):
        return pl.ds((d * TILE + i) * cols + j, wide, stride=TILE)

    def place(i, j):
        return pl.ds(pl.multiple_of((i * TILE + j) * 8, 8), 8)

    def gather(i, carry):
        for j in range(TILE):
            v = jnp.concatenate([field[source(i, j, d)] for d in range(down)], axis=0)
            t_a[place(i, j)] = v
            gain[place(i, j)] = (0.3 * v) * lax.rsqrt(v * v + 1.0)
            sign[place(i, j)] = jnp.where(v > 0.0, 1.0, -1.0)
        return carry

    lax.fori_loop(0, TILE, gather, 0)

    def sweep(now, later):
        zero = jnp.zeros((8, 128), jnp.float32)
        above = [zero] * TILE
        values = [now[place(0, j)] for j in range(TILE)]
        for i in range(TILE):
            next_values = [now[place(i + 1, j)] for j in range(TILE)] if i + 1 < TILE else values
            left = zero
            next_above = []
            for j in range(TILE):
                v = values[j]
                s = sign[place(i, j)]
                below = next_values[j] - v
                right = values[j + 1] - v if j + 1 < TILE else zero
                back = (v - pltpu.roll(v, 1, 1)) * inner
                total = None
                for m, q in ((above[j], below), (left, right), (back, pltpu.roll(back, 127, 1))):
                    floor = FLOOR if total is None else 0.0
                    u = jnp.maximum(jnp.maximum(s * m, -s * q), floor)
                    total = u * u if total is None else total + u * u
                later[place(i, j)] = v - gain[place(i, j)] * (total * lax.rsqrt(total) - 1.0)
                next_above.append(below)
                left = right
            above, values = next_above, next_values

    def sweeps(index, carry):
        sweep(t_a, t_b)
        sweep(t_b, t_a)
        return carry

    lax.fori_loop(0, REINIT // 2, sweeps, 0)

    def copy_out(i, d):
        at = pl.ds(pl.multiple_of((d * TILE + i) * cols, 8), cols)
        return pltpu.make_async_copy(merged.at[at], out.at[at], store_sem.at[d * TILE + i])

    def scatter(i, carry):
        for j in range(TILE):
            v = t_a[place(i, j)]
            for d in range(down):
                at = source(i, j, d)
                part = slice(d * wide, (d + 1) * wide)
                merged[at] = jnp.where(chosen[part] > 0, v[part], field[at])
        for d in range(down):
            copy_out(i, d).start()
        return carry

    lax.fori_loop(0, TILE, scatter, 0)

    def finish(i, carry):
        for d in range(down):
            copy_out(i, d).wait()
        return carry

    lax.fori_loop(0, TILE, finish, 0)


def reinitialize(field, band, rows, cols):
    cells = rows * cols
    flat = pltpu.VMEM((cells, 128), jnp.float32)
    return pl.pallas_call(
        functools.partial(reinit_kernel, rows, cols),
        out_shape=jax.ShapeDtypeStruct((cells, 128), jnp.float32),
        in_specs=[
            pl.BlockSpec(memory_space=pltpu.VMEM),
            pl.BlockSpec(memory_space=pltpu.SMEM),
        ],
        out_specs=pl.BlockSpec(memory_space=pltpu.HBM),
        scratch_shapes=[flat, flat, flat, flat, pltpu.SemaphoreType.DMA((rows,)), flat],
        compiler_params=pltpu.CompilerParams(vmem_limit_bytes=24 * 2**20),
        name="reinitialize",
    )(field, band)


def solution(mesh):
    n_gx, n_gy = mesh.shape["gx"], mesh.shape["gy"]

    def body(level_set, normal_speed, band_tiles):
        rows, cols, depth = level_set.shape
        cells = rows * cols
        field = advance(
            level_set.reshape(cells, depth), normal_speed.reshape(cells, depth),
            rows, cols, n_gx, n_gy,
        )
        return reinitialize(field, band_tiles, rows, cols).reshape(rows, cols, depth)

    return jax.shard_map(
        body,
        mesh=mesh,
        in_specs=(
            P(("groups", "gx"), "gy", None),
            P(("groups", "gx"), "gy", None),
            P(("groups", "gx"), "gy"),
        ),
        out_specs=P(("groups", "gx"), "gy", None),
        check_vma=False,
    )
```

time: 80.7 us -> 51.9 us (0.64)
  the two profiles are of different devices: /device:TPU:17 before, /device:TPU:21 now
where the time goes in v3:
time: 51.9 us; the launch traced here: 51.7 us
  Pallas kernels  49.2 us (95%)
  local copies, waits for them, and re-layouts  2.45 us (5%)
    pallas_call x1, Pallas kernels, advance(): pl.pallas_call(functools.partial(advance_kernel, rows, cols, n_gx, n_gy),...  34.8 us
    pallas_call x1, Pallas kernels, reinitialize(): pl.pallas_call(functools.partial(reinit_kernel, rows, cols), out_shape=ja...  14.4 us
    unnamed x6, local copies, waits for them, and re-layouts  2.45 us

profile of v3, /device:TPU:21, one launch (start us, length us, event | category | flops | bytes accessed | tf_op | source)
XLA Modules:
  0.0 51.7 jit_solution(15428460174764988782)
XLA Ops:
  0.0 0.0 copy-start
  0.0 1.2 %copy-done = f32[32,64,128]{2,1,0:T(8,128)S(1)} copy-done((f32[32,64,128]{2,1,0:T(8,128)S(1)}, f32[32,64,128]{2,1,0:T(8,128)}, u32[]{:S(2)}) %copy-start) | copy-done | bytes 1048600
  1.2 0.0 copy-start.1
  1.2 1.2 %copy-done.1 = f32[32,64,128]{2,1,0:T(8,128)S(1)} copy-done((f32[32,64,128]{2,1,0:T(8,128)S(1)}, f32[32,64,128]{2,1,0:T(8,128)}, u32[]{:S(2)}) %copy-start.1) | copy-done | bytes 1048600
  2.5 0.0 copy-start.2
  2.5 34.8 %advance.1.field = f32[2048,128]{1,0:T(8,128)S(1)} custom-call(f32[2048,128]{1,0:T(8,128)S(1)} %bitcast.3, f32[2048,128]{1,0:T(8,128)S(1)} %bitcast.4), custom_call_target="tpu_custom_call" | custom-call | tf_op jit(solution)/shard_map/advance/pallas_call | solution.py:371
  37.2 0.0 copy-done.2
  37.2 14.4 %reinitialize.1 = f32[2048,128]{1,0:T(8,128)} custom-call(f32[2048,128]{1,0:T(8,128)S(1)} %advance.1.field, s32[2,4]{1,0:T(2,128)S(1)} %copy-done.2), custom_call_target="tpu_custom_call" | custom-call | tf_op jit(solution)/shard_map/reinitialize/pallas_call | solution.py:480
Async XLA Ops:
  0.0 1.2 %copy-start = (f32[32,64,128]{2,1,0:T(8,128)S(1)}, f32[32,64,128]{2,1,0:T(8,128)}, u32[]{:S(2)}) copy-start(f32[32,64,128]{2,1,0:T(8,128)} %param.3) | copy-start | bytes 3145732
  1.2 1.2 %copy-start.1 = (f32[32,64,128]{2,1,0:T(8,128)S(1)}, f32[32,64,128]{2,1,0:T(8,128)}, u32[]{:S(2)}) copy-start(f32[32,64,128]{2,1,0:T(8,128)} %param.4) | copy-start | bytes 3145732
  2.5 34.8 %copy-start.2 = (s32[2,4]{1,0:T(2,128)S(1)}, s32[2,4]{1,0:T(2,128)}, u32[]{:S(2)}) copy-start(s32[2,4]{1,0:T(2,128)} %band.1) | copy-start | bytes 100

commit v4 on v3

--- a/solution.py
+++ b/solution.py
@@ -21,9 +21,8 @@
 OUT_PITCH = 132
 ZPAD = 4
 GAP = 8
-Z_STEPS = 32
-Y_TRIPS = 2
-PARTS = 4
+Z_STEPS = 64
+CHUNKS = 4
 MESH = pl.DeviceIdType.MESH
 
 
@@ -83,17 +82,18 @@
 
 def advance_kernel(
     rows, cols, n_gx, n_gy,
-    level_hbm, speed_hbm, out_ref,
-    field_a, field_b, kept, speed, rate, sign, acc_y, acc_z, zin, zout, zsign, yface, yhalo,
-    send_sem, recv_sem, local_sem,
+    level, speed, out_ref,
+    field_a, field_b, kept, rate, sign, acc_y, acc_z, zin, zout, zsign,
+    xface, xhalo, yface, yhalo, x_send, x_recv, y_send, y_recv,
 ):
     cells = rows * cols
     pitch = cols + GAP
-    own = GHOST * pitch
     blocks = cells // 128
     block_rows = 128 // cols
     groups = blocks // 8
     face = GHOST * rows
+    slab = cols // CHUNKS
+    xface_rows = GHOST * slab
     gx = lax.axis_index("gx")
     gy = lax.axis_index("gy")
     low_x, high_x = gx > 0, gx < n_gx - 1
@@ -103,47 +103,25 @@
         (low_y, {"gy": gy - 1}), (high_y, {"gy": gy + 1}),
     )
 
-    part = cells // PARTS
-    loads = []
-    for n in range(PARTS):
-        at = pl.ds(n * part, part)
-        loads.append((
-            pltpu.make_async_copy(level_hbm.at[at], acc_z.at[at], local_sem.at[n]),
-            pltpu.make_async_copy(speed_hbm.at[at], speed.at[at], local_sem.at[PARTS + n]),
-        ))
-    for level, _ in loads:
-        level.start()
-    for _, moving in loads:
-        moving.start()
-
     barrier = pltpu.get_barrier_semaphore()
     for there, device in sides:
         @pl.when(there)
         def _():
             pl.semaphore_signal(barrier, inc=1, device_id=device, device_id_type=MESH)
 
-    zero = jnp.zeros((own, 128), jnp.float32)
     gap = jnp.zeros((GAP, 128), jnp.float32)
-    for field in (field_a, field_b):
-        for x in range(rows):
-            field[pl.ds(own + x * pitch + cols, GAP)] = gap
-
-        @pl.when(jnp.logical_not(low_x))
-        def _():
-            field[pl.ds(0, own)] = zero
-
-        @pl.when(jnp.logical_not(high_x))
-        def _():
-            field[pl.ds(own + rows * pitch, own)] = zero
-
+    x_zero = jnp.zeros((CHUNKS * xface_rows, 128), jnp.float32)
+    y_zero = jnp.zeros((face, 128), jnp.float32)
     for stage in range(STAGES):
-        @pl.when(jnp.logical_not(low_y))
-        def _():
-            yhalo[pl.ds((stage * 2) * face, face)] = zero[:face]
-
-        @pl.when(jnp.logical_not(high_y))
-        def _():
-            yhalo[pl.ds((stage * 2 + 1) * face, face)] = zero[:face]
+        for side, (there, _) in enumerate(sides[:2]):
+            @pl.when(jnp.logical_not(there))
+            def _(at=(stage * 2 + side) * CHUNKS * xface_rows):
+                xhalo[pl.ds(at, CHUNKS * xface_rows)] = x_zero
+
+        for side, (there, _) in enumerate(sides[2:]):
+            @pl.when(jnp.logical_not(there))
+            def _(at=(stage * 2 + side) * face):
+                yhalo[pl.ds(at, face)] = y_zero
 
     for q in range(groups):
         for block in range(8):
@@ -157,18 +135,58 @@
     def spaced(x, y):
         return pl.ds(pl.multiple_of(x * pitch + y, 8), 8)
 
-    for level, _ in loads:
-        level.wait()
+    def x_at(stage, side, chunk):
+        return ((stage * 2 + side) * CHUNKS + chunk) * xface_rows
+
+    def x_copy(stage, side, chunk):
+        sem = (stage * 2 + side) * CHUNKS + chunk
+        return pltpu.make_async_remote_copy(
+            src_ref=xface.at[pl.ds(pl.multiple_of(x_at(stage, side, chunk), 8), xface_rows)],
+            dst_ref=xhalo.at[pl.ds(pl.multiple_of(x_at(stage, 1 - side, chunk), 8), xface_rows)],
+            send_sem=x_send.at[sem],
+            recv_sem=x_recv.at[sem],
+            device_id=sides[side][1],
+            device_id_type=MESH,
+        )
+
+    def y_copy(stage, side):
+        return pltpu.make_async_remote_copy(
+            src_ref=yface.at[pl.ds((stage * 2 + side) * face, face)],
+            dst_ref=yhalo.at[pl.ds((stage * 2 + 1 - side) * face, face)],
+            send_sem=y_send.at[stage * 2 + side],
+            recv_sem=y_recv.at[stage * 2 + side],
+            device_id=sides[2 + side][1],
+            device_id_type=MESH,
+        )
+
+    def x_start(field, stage, chunk):
+        for side in range(2):
+            for n in range(GHOST):
+                x = n if side == 0 else rows - GHOST + n
+                for y in range(0, slab, 8):
+                    at = pl.multiple_of(x_at(stage, side, chunk) + n * slab + y, 8)
+                    xface[pl.ds(at, 8)] = field[spaced(x, chunk * slab + y)]
+        for side in range(2):
+            @pl.when(sides[side][0])
+            def _(side=side):
+                x_copy(stage, side, chunk).start()
 
     def scaled(x, carry):
-        field_a[pl.ds(pl.multiple_of(own + x * pitch, 8), cols)] = (
-            acc_z[pl.ds(pl.multiple_of(x * cols, 8), cols)] * SCALE
+        field_a[pl.ds(pl.multiple_of(x * pitch, 8), cols)] = (
+            level[pl.ds(pl.multiple_of(x * cols, 8), cols)] * SCALE
         )
         return carry
 
     lax.fori_loop(0, rows, scaled, 0, unroll=True)
-    for _, moving in loads:
-        moving.wait()
+
+    there_count = sum(there.astype(jnp.int32) for there, _ in sides)
+    pl.semaphore_wait(barrier, there_count)
+
+    def first_chunk(chunk, carry):
+        x_start(field_a, 0, chunk)
+        return carry
+
+    lax.fori_loop(0, CHUNKS, first_chunk, 0)
 
     def signs(block, carry):
         here = pl.ds(pl.multiple_of(block * 128, 128), 128)
@@ -187,46 +205,24 @@
 
         lax.fori_loop(0, 8, sign_block, 0, unroll=True)
 
-    there_count = sum(there.astype(jnp.int32) for there, _ in sides)
-    pl.semaphore_wait(barrier, there_count)
-
-    def one_stage(stage, field, write):
-        sends = []
-        for direction, (src, src_at, dst, dst_at, count) in enumerate((
-            (field, own, field, own + rows * pitch, own),
-            (field, rows * pitch, field, 0, own),
-            (yface, (stage * 2) * face, yhalo, (stage * 2 + 1) * face, face),
-            (yface, (stage * 2 + 1) * face, yhalo, (stage * 2) * face, face),
-        )):
-            sends.append(pltpu.make_async_remote_copy(
-                src_ref=src.at[pl.ds(src_at, count)],
-                dst_ref=dst.at[pl.ds(dst_at, count)],
-                send_sem=send_sem.at[stage * 4 + direction],
-                recv_sem=recv_sem.at[stage * 4 + direction],
-                device_id=sides[direction][1],
-                device_id_type=MESH,
-            ))
-        for direction in (0, 1):
-            @pl.when(sides[direction][0])
-            def _(direction=direction):
-                sends[direction].start()
+    def one_stage(stage, field, fresh, write, more):
         for side in range(2):
             for n in range(GHOST):
                 y = n if side == 0 else cols - GHOST + n
                 for x in range(0, rows, 8):
                     yface[pl.ds((stage * 2 + side) * face + n * rows + x, 8)] = field[
-                        pl.ds(own + x * pitch + y, 8, stride=pitch)
+                        pl.ds(x * pitch + y, 8, stride=pitch)
                     ]
-        for direction in (2, 3):
-            @pl.when(sides[direction][0])
-            def _(direction=direction):
-                sends[direction].start()
+        for side in range(2):
+            @pl.when(sides[2 + side][0])
+            def _(side=side):
+                y_copy(stage, side).start()
 
         def flip(q, block):
             v = []
             for n in range(block_rows):
                 x = (q * 8 + block) * block_rows + n
-                v.append(field[pl.ds(pl.multiple_of(own + x * pitch, 8), cols)])
+                v.append(field[pl.ds(pl.multiple_of(x * pitch, 8), cols)])
             zin[q][pl.ds(block * PITCH + ZPAD, 128)] = jnp.concatenate(v, axis=0).T
 
         def unflip(q, block):
@@ -263,10 +259,10 @@
             first = push(begin([z_cell(z) for z in range(-3, 2)]), z_cell(2))
             lax.fori_loop(0, trips, z_trip, first[:2])
 
-        for direction, there in ((2, high_y), (3, low_y)):
-            @pl.when(there)
-            def _(direction=direction):
-                sends[direction].wait_recv()
+        for side in range(2):
+            @pl.when(sides[2 + side][0])
+            def _(side=side):
+                y_copy(stage, 1 - side).wait_recv()
 
         def y_block(block, carry):
             x = block * 8
@@ -278,7 +274,7 @@
                 return yhalo[pl.ds(pl.multiple_of((stage * 2 + 1) * face + n * rows + x, 8), 8)]
 
             def cell(y):
-                return field[pl.ds(own + x * pitch + y, 8, stride=pitch)]
+                return field[pl.ds(x * pitch + y, 8, stride=pitch)]
 
             def step(y, carry, phi):
                 st, behind = carry
@@ -289,58 +285,56 @@
 
             st = begin([low_cell(n) for n in range(GHOST)] + [cell(0), cell(1)])
             carried = push(st, cell(2))[:2]
-            count = (cols - GHOST) // Y_TRIPS
-
-            def y_trip(trip, carried):
-                unflip(groups - 1, block * Y_TRIPS + trip)
-                start = trip * count
-                return lax.fori_loop(
-                    0, count,
-                    lambda u, c: step(start + u, c, cell(start + u + GHOST)),
-                    carried, unroll=True,
-                )
-
-            carried = lax.fori_loop(0, Y_TRIPS, y_trip, carried)
-            for y in range(count * Y_TRIPS, cols):
-                ahead = y + GHOST
-                phi = cell(ahead) if ahead < cols else high_cell(ahead - cols)
-                carried = step(y, carried, phi)
+            for n in range(8 // (rows // 8)):
+                unflip(groups - 1, block * (8 // (rows // 8)) + n)
+            carried = lax.fori_loop(
+                0, cols - GHOST, lambda y, c: step(y, c, cell(y + GHOST)), carried, unroll=True
+            )
+            for n in range(GHOST):
+                carried = step(cols - GHOST + n, carried, high_cell(n))
             return carry
 
         lax.fori_loop(0, rows // 8, y_block, 0)
 
-        for direction, there in ((0, high_x), (1, low_x)):
-            @pl.when(there)
-            def _(direction=direction):
-                sends[direction].wait_recv()
-
-        def x_block(block, carry):
-            y = block * 8
-
+        def x_block(chunk, y):
             def cell(x):
-                return field[spaced(x + GHOST, y)]
-
-            st = begin([cell(x) for x in range(-3, 2)])
-            carried = push(st, cell(2))[:2]
-
-            def step(x, carry):
+                return field[spaced(x, chunk * slab + y)]
+
+            def ghost(side, n):
+                at = x_at(stage, side, chunk) + n * slab + y
+                return xhalo[pl.ds(pl.multiple_of(at, 8), 8)]
+
+            def step(x, carry, phi):
                 st, behind = carry
-                st, next_behind, ahead = push(st, cell(x + 3))
-                at, here = spaced(x, y), natural(x, y)
+                st, next_behind, ahead = push(st, phi)
+                at, here = spaced(x, chunk * slab + y), natural(x, chunk * slab + y)
                 total = upwind(sign[at], behind, ahead) + (acc_y[at] + acc_z[here])
                 now = cell(x)
-                write(now, now - rate[here] * root(total), spaced(x + GHOST, y), here)
+                write(now, now - rate[here] * root(total), at, here)
                 return st, next_behind
 
-            lax.fori_loop(0, rows, step, carried, unroll=True)
+            st = begin([ghost(0, n) for n in range(GHOST)] + [cell(0), cell(1)])
+            carried = push(st, cell(2))[:2]
+            carried = lax.fori_loop(
+                0, rows - GHOST, lambda x, c: step(x, c, cell(x + GHOST)), carried, unroll=True
+            )
+            for n in range(GHOST):
+                carried = step(rows - GHOST + n, carried, ghost(1, n))
+
+        def x_chunk(chunk, carry):
+            for side in range(2):
+                @pl.when(sides[side][0])
+                def _(side=side):
+                    x_copy(stage, 1 - side, chunk).wait_recv()
+            for y in range(0, slab, 8):
+                x_block(chunk, y)
+
+            @pl.when(more)
+            def _():
+                x_start(fresh, stage + 1, chunk)
             return carry
 
-        lax.fori_loop(0, cols // 8, x_block, 0)
-
-        for direction in range(4):
-            @pl.when(sides[direction][0])
-            def _(direction=direction):
-                sends[direction].wait_send()
+        lax.fori_loop(0, CHUNKS, x_chunk, 0)
 
     def time_step(step, carry):
         last = jnp.where(step == RK_STEPS - 1, jnp.float32(0.5 / SCALE), jnp.float32(0.5))
@@ -354,11 +348,25 @@
             field_a[at] = result
             out_ref[here] = result
 
-        one_stage(2 * step, field_a, halfway)
-        one_stage(2 * step + 1, field_b, whole)
+        one_stage(2 * step, field_a, field_b, halfway, True)
+        one_stage(2 * step + 1, field_b, field_a, whole, step < RK_STEPS - 1)
         return carry
 
     lax.fori_loop(0, RK_STEPS, time_step, 0)
+
+    def sent(stage, carry):
+        for side in range(2):
+            @pl.when(sides[side][0])
+            def _(side=side):
+                for chunk in range(CHUNKS):
+                    x_copy(stage, side, chunk).wait_send()
+
+            @pl.when(sides[2 + side][0])
+            def _(side=side):
+                y_copy(stage, side).wait_send()
+        return carry
+
+    lax.fori_loop(0, STAGES, sent, 0)
 
 
 def advance(level_set, normal_speed, rows, cols, n_gx, n_gy):
@@ -367,22 +375,24 @@
     pitch = cols + GAP
     flat = pltpu.VMEM((cells, 128), jnp.float32)
     spaced = pltpu.VMEM((rows * pitch, 128), jnp.float32)
-    padded = pltpu.VMEM(((rows + 2 * GHOST) * pitch, 128), jnp.float32)
     return pl.pallas_call(
         functools.partial(advance_kernel, rows, cols, n_gx, n_gy),
         out_shape=jax.ShapeDtypeStruct((cells, 128), jnp.float32),
-        in_specs=[pl.BlockSpec(memory_space=pltpu.HBM)] * 2,
+        in_specs=[pl.BlockSpec(memory_space=pltpu.VMEM)] * 2,
         out_specs=pl.BlockSpec(memory_space=pltpu.VMEM),
         scratch_shapes=[
-            padded, padded, flat, flat, flat, spaced, spaced, flat,
+            spaced, spaced, flat, flat, spaced, spaced, flat,
             [pltpu.VMEM((8 * PITCH, 128), jnp.float32)] * groups,
             [pltpu.VMEM((8 * OUT_PITCH, 128), jnp.float32)] * groups,
             [pltpu.VMEM((8 * OUT_PITCH, 128), jnp.float32)] * groups,
+            pltpu.VMEM((STAGES * 2 * GHOST * cols, 128), jnp.float32),
+            pltpu.VMEM((STAGES * 2 * GHOST * cols, 128), jnp.float32),
             pltpu.VMEM((STAGES * 2 * GHOST * rows, 128), jnp.float32),
             pltpu.VMEM((STAGES * 2 * GHOST * rows, 128), jnp.float32),
-            pltpu.SemaphoreType.DMA((STAGES * 4,)),
-            pltpu.SemaphoreType.DMA((STAGES * 4,)),
-            pltpu.SemaphoreType.DMA((2 * PARTS,)),
+            pltpu.SemaphoreType.DMA((STAGES * 2 * CHUNKS,)),
+            pltpu.SemaphoreType.DMA((STAGES * 2 * CHUNKS,)),
+            pltpu.SemaphoreType.DMA((STAGES * 2,)),
+            pltpu.SemaphoreType.DMA((STAGES * 2,)),
         ],
         compiler_params=pltpu.CompilerParams(
             collective_id=0, has_side_effects=True, vmem_limit_bytes=28 * 2**20

time: 51.9 us -> 44.6 us (0.86)
  the two profiles are of different devices: /device:TPU:21 before, /device:TPU:0 now
where the time goes in v4:
time: 44.6 us; the launch traced here: 44.4 us
  Pallas kernels  41.9 us (94%)
  local copies, waits for them, and re-layouts  2.45 us (5%)
    pallas_call x1, Pallas kernels, advance(): pl.pallas_call(functools.partial(advance_kernel, rows, cols, n_gx, n_gy),...  27.5 us
    pallas_call x1, Pallas kernels, reinitialize(): pl.pallas_call(functools.partial(reinit_kernel, rows, cols), out_shape=ja...  14.4 us
    unnamed x6, local copies, waits for them, and re-layouts  2.45 us

profile of v4, /device:TPU:0, one launch (start us, length us, event | category | flops | bytes accessed | tf_op | source)
XLA Modules:
  0.0 44.4 jit_solution(17670069278288574123)
XLA Ops:
  0.0 0.0 copy-start
  0.0 1.2 %copy-done = f32[32,64,128]{2,1,0:T(8,128)S(1)} copy-done((f32[32,64,128]{2,1,0:T(8,128)S(1)}, f32[32,64,128]{2,1,0:T(8,128)}, u32[]{:S(2)}) %copy-start) | copy-done | bytes 1048600
  1.2 0.0 copy-start.1
  1.2 1.2 %copy-done.1 = f32[32,64,128]{2,1,0:T(8,128)S(1)} copy-done((f32[32,64,128]{2,1,0:T(8,128)S(1)}, f32[32,64,128]{2,1,0:T(8,128)}, u32[]{:S(2)}) %copy-start.1) | copy-done | bytes 1048600
  2.5 0.0 copy-start.2
  2.5 27.5 %advance.1.field = f32[2048,128]{1,0:T(8,128)S(1)} custom-call(f32[2048,128]{1,0:T(8,128)S(1)} %bitcast.3, f32[2048,128]{1,0:T(8,128)S(1)} %bitcast.4), custom_call_target="tpu_custom_call" | custom-call | tf_op jit(solution)/shard_map/advance/pallas_call | solution.py:378
  30.0 0.0 copy-done.2
  30.0 14.4 %reinitialize.1 = f32[2048,128]{1,0:T(8,128)} custom-call(f32[2048,128]{1,0:T(8,128)S(1)} %advance.1.field, s32[2,4]{1,0:T(2,128)S(1)} %copy-done.2), custom_call_target="tpu_custom_call" | custom-call | tf_op jit(solution)/shard_map/reinitialize/pallas_call | solution.py:490
Async XLA Ops:
  0.0 1.2 %copy-start = (f32[32,64,128]{2,1,0:T(8,128)S(1)}, f32[32,64,128]{2,1,0:T(8,128)}, u32[]{:S(2)}) copy-start(f32[32,64,128]{2,1,0:T(8,128)} %param.3) | copy-start | bytes 3145732
  1.2 1.2 %copy-start.1 = (f32[32,64,128]{2,1,0:T(8,128)S(1)}, f32[32,64,128]{2,1,0:T(8,128)}, u32[]{:S(2)}) copy-start(f32[32,64,128]{2,1,0:T(8,128)} %param.4) | copy-start | bytes 3145732
  2.5 27.5 %copy-start.2 = (s32[2,4]{1,0:T(2,128)S(1)}, s32[2,4]{1,0:T(2,128)}, u32[]{:S(2)}) copy-start(s32[2,4]{1,0:T(2,128)} %band.1) | copy-start | bytes 100

commit v5 on v4

--- a/solution.py
+++ b/solution.py
@@ -78,6 +78,12 @@
 def upwind(sign, behind, ahead):
     v = jnp.maximum(jnp.maximum(sign * behind, sign * ahead), 0.0)
     return v * v
+
+
+def by_tile(x, y, cols):
+    i, j = lax.rem(x, TILE), lax.rem(y, TILE)
+    slot = (x // TILE) * (cols // TILE) + y // TILE
+    return pl.ds((i * TILE + j) * 8 + slot, 8, stride=8)
 
 
 def advance_kernel(
@@ -310,7 +316,10 @@
                 at, here = spaced(x, chunk * slab + y), natural(x, chunk * slab + y)
                 total = upwind(sign[at], behind, ahead) + (acc_y[at] + acc_z[here])
                 now = cell(x)
-                write(now, now - rate[here] * root(total), at, here)
+                write(
+                    now, now - rate[here] * root(total), at, here,
+                    by_tile(x, chunk * slab + y, cols),
+                )
                 return st, next_behind
 
             st = begin([ghost(0, n) for n in range(GHOST)] + [cell(0), cell(1)])
@@ -339,14 +348,14 @@
     def time_step(step, carry):
         last = jnp.where(step == RK_STEPS - 1, jnp.float32(0.5 / SCALE), jnp.float32(0.5))
 
-        def halfway(now, moved, at, here):
+        def halfway(now, moved, at, here, tiled):
             field_b[at] = moved
             kept[here] = now
 
-        def whole(now, moved, at, here):
+        def whole(now, moved, at, here, tiled):
             result = last * (kept[here] + moved)
             field_a[at] = result
-            out_ref[here] = result
+            out_ref[tiled] = result
 
         one_stage(2 * step, field_a, field_b, halfway, True)
         one_stage(2 * step + 1, field_b, field_a, whole, step < RK_STEPS - 1)
@@ -401,7 +410,7 @@
     )(level_set, normal_speed)
 
 
-def reinit_kernel(rows, cols, field, band, out, t_a, t_b, gain, sign, store_sem, merged):
+def reinit_kernel(rows, cols, start, band, out, t_a, t_b, gain, sign, store_sem, merged):
     wide = cols // TILE
     down = rows // TILE
     lane = lax.broadcasted_iota(jnp.int32, (8, 128), 1)
@@ -412,21 +421,17 @@
         for w in range(wide):
             chosen = jnp.where(slot == d * wide + w, band[d, w], chosen)
 
-    def source(i, j, d):
-        return pl.ds((d * TILE + i) * cols + j, wide, stride=TILE)
-
     def place(i, j):
         return pl.ds(pl.multiple_of((i * TILE + j) * 8, 8), 8)
 
     def gather(i, carry):
         for j in range(TILE):
-            v = jnp.concatenate([field[source(i, j, d)] for d in range(down)], axis=0)
-            t_a[place(i, j)] = v
-            gain[place(i, j)] = (0.3 * v) * lax.rsqrt(v * v + 1.0)
+            v = start[place(i, j)]
+            gain[place(i, j)] = jnp.where(chosen > 0, (0.3 * v) * lax.rsqrt(v * v + 1.0), 0.0)
             sign[place(i, j)] = jnp.where(v > 0.0, 1.0, -1.0)
         return carry
 
-    lax.fori_loop(0, TILE, gather, 0)
+    lax.fori_loop(0, TILE, gather, 0, unroll=2)
 
     def sweep(now, later):
         zero = jnp.zeros((8, 128), jnp.float32)
@@ -457,19 +462,19 @@
         sweep(t_b, t_a)
         return carry
 
-    lax.fori_loop(0, REINIT // 2, sweeps, 0)
+    sweep(start, t_b)
+    sweep(t_b, t_a)
+    lax.fori_loop(0, REINIT // 2 - 1, sweeps, 0)
 
     def copy_out(i, d):
         at = pl.ds(pl.multiple_of((d * TILE + i) * cols, 8), cols)
         return pltpu.make_async_copy(merged.at[at], out.at[at], store_sem.at[d * TILE + i])
 
     def scatter(i, carry):
-        for j in range(TILE):
-            v = t_a[place(i, j)]
-            for d in range(down):
-                at = source(i, j, d)
-                part = slice(d * wide, (d + 1) * wide)
-                merged[at] = jnp.where(chosen[part] > 0, v[part], field[at])
+        for d in range(down):
+            for y in range(0, cols, 8):
+                at = pl.ds(pl.multiple_of((d * TILE + i) * cols + y, 8), 8)
+                merged[at] = t_a[by_tile(d * TILE + i, y, cols)]
         for d in range(down):
             copy_out(i, d).start()
         return carry

time: 44.6 us -> 44 us (0.987)
  Pallas kernels: 41.9 us -> 41.4 us
    pallas_call x1, Pallas kernels: 14.4 us -> 13.7 us  [reinitialize(): pl.pallas_call(functools.partial(reinit_kernel, rows, cols), out_shape=ja...]
where the time goes in v5:
time: 44 us; the launch traced here: 43.9 us
  Pallas kernels  41.4 us (94%)
  local copies, waits for them, and re-layouts  2.45 us (6%)
    pallas_call x1, Pallas kernels, advance(): pl.pallas_call(functools.partial(advance_kernel, rows, cols, n_gx, n_gy),...  27.6 us
    pallas_call x1, Pallas kernels, reinitialize(): pl.pallas_call(functools.partial(reinit_kernel, rows, cols), out_shape=ja...  13.7 us
    unnamed x6, local copies, waits for them, and re-layouts  2.45 us

profile of v5, /device:TPU:0, one launch (start us, length us, event | category | flops | bytes accessed | tf_op | source)
XLA Modules:
  0.0 43.9 jit_solution(16617196294747370450)
XLA Ops:
  0.0 0.0 copy-start
  0.0 1.2 %copy-done = f32[32,64,128]{2,1,0:T(8,128)S(1)} copy-done((f32[32,64,128]{2,1,0:T(8,128)S(1)}, f32[32,64,128]{2,1,0:T(8,128)}, u32[]{:S(2)}) %copy-start) | copy-done | bytes 1048600
  1.2 0.0 copy-start.1
  1.2 1.2 %copy-done.1 = f32[32,64,128]{2,1,0:T(8,128)S(1)} copy-done((f32[32,64,128]{2,1,0:T(8,128)S(1)}, f32[32,64,128]{2,1,0:T(8,128)}, u32[]{:S(2)}) %copy-start.1) | copy-done | bytes 1048600
  2.5 0.0 copy-start.2
  2.5 27.6 %advance.1.start = f32[2048,128]{1,0:T(8,128)S(1)} custom-call(f32[2048,128]{1,0:T(8,128)S(1)} %bitcast.3, f32[2048,128]{1,0:T(8,128)S(1)} %bitcast.4), custom_call_target="tpu_custom_call" | custom-call | tf_op jit(solution)/shard_map/advance/pallas_call | solution.py:387
  30.1 0.0 copy-done.2
  30.1 13.7 %reinitialize.1 = f32[2048,128]{1,0:T(8,128)} custom-call(f32[2048,128]{1,0:T(8,128)S(1)} %advance.1.start, s32[2,4]{1,0:T(2,128)S(1)} %copy-done.2), custom_call_target="tpu_custom_call" | custom-call | tf_op jit(solution)/shard_map/reinitialize/pallas_call | solution.py:495
Async XLA Ops:
  0.0 1.2 %copy-start = (f32[32,64,128]{2,1,0:T(8,128)S(1)}, f32[32,64,128]{2,1,0:T(8,128)}, u32[]{:S(2)}) copy-start(f32[32,64,128]{2,1,0:T(8,128)} %param.3) | copy-start | bytes 3145732
  1.2 1.2 %copy-start.1 = (f32[32,64,128]{2,1,0:T(8,128)S(1)}, f32[32,64,128]{2,1,0:T(8,128)}, u32[]{:S(2)}) copy-start(f32[32,64,128]{2,1,0:T(8,128)} %param.4) | copy-start | bytes 3145732
  2.5 27.7 %copy-start.2 = (s32[2,4]{1,0:T(2,128)S(1)}, s32[2,4]{1,0:T(2,128)}, u32[]{:S(2)}) copy-start(s32[2,4]{1,0:T(2,128)} %band.1) | copy-start | bytes 100

commit v6 on v5

--- a/solution.py
+++ b/solution.py
@@ -410,11 +410,12 @@
     )(level_set, normal_speed)
 
 
-def reinit_kernel(rows, cols, start, band, out, t_a, t_b, gain, sign, store_sem, merged):
+def reinit_kernel(rows, cols, start, band, out, t_a, t_b, gain, sign, minus, sign_low, minus_high, store_sem, merged):
     wide = cols // TILE
     down = rows // TILE
     lane = lax.broadcasted_iota(jnp.int32, (8, 128), 1)
-    inner = jnp.where(lane == 0, 0.0, 1.0)
+    not_first = lane > 0
+    not_last = lane < 127
     slot = lax.broadcasted_iota(jnp.int32, (8, 128), 0)
     chosen = jnp.zeros((8, 128), jnp.int32)
     for d in range(down):
@@ -428,7 +429,11 @@
         for j in range(TILE):
             v = start[place(i, j)]
             gain[place(i, j)] = jnp.where(chosen > 0, (0.3 * v) * lax.rsqrt(v * v + 1.0), 0.0)
-            sign[place(i, j)] = jnp.where(v > 0.0, 1.0, -1.0)
+            s = jnp.where(v > 0.0, 1.0, -1.0)
+            sign[place(i, j)] = s
+            minus[place(i, j)] = -s
+            sign_low[place(i, j)] = jnp.where(not_first, s, 0.0)
+            minus_high[place(i, j)] = jnp.where(not_last, -s, 0.0)
         return carry
 
     lax.fori_loop(0, TILE, gather, 0, unroll=2)
@@ -443,14 +448,19 @@
             next_above = []
             for j in range(TILE):
                 v = values[j]
-                s = sign[place(i, j)]
+                s, ns = sign[place(i, j)], minus[place(i, j)]
                 below = next_values[j] - v
                 right = values[j + 1] - v if j + 1 < TILE else zero
-                back = (v - pltpu.roll(v, 1, 1)) * inner
+                back = v - pltpu.roll(v, 1, 1)
+                ahead = pltpu.roll(back, 127, 1)
                 total = None
-                for m, q in ((above[j], below), (left, right), (back, pltpu.roll(back, 127, 1))):
+                for sm, sq in (
+                    (s * above[j], ns * below),
+                    (s * left, ns * right),
+                    (sign_low[place(i, j)] * back, minus_high[place(i, j)] * ahead),
+                ):
                     floor = FLOOR if total is None else 0.0
-                    u = jnp.maximum(jnp.maximum(s * m, -s * q), floor)
+                    u = jnp.maximum(jnp.maximum(sm, sq), floor)
                     total = u * u if total is None else total + u * u
                 later[place(i, j)] = v - gain[place(i, j)] * (total * lax.rsqrt(total) - 1.0)
                 next_above.append(below)
@@ -500,7 +510,7 @@
             pl.BlockSpec(memory_space=pltpu.SMEM),
         ],
         out_specs=pl.BlockSpec(memory_space=pltpu.HBM),
-        scratch_shapes=[flat, flat, flat, flat, pltpu.SemaphoreType.DMA((rows,)), flat],
+        scratch_shapes=[flat] * 7 + [pltpu.SemaphoreType.DMA((rows,)), flat],
         compiler_params=pltpu.CompilerParams(vmem_limit_bytes=24 * 2**20),
         name="reinitialize",
     )(field, band)

time: 44 us -> 43.4 us (0.986)
  Pallas kernels: 41.4 us -> 40.8 us
    pallas_call x1, Pallas kernels: 13.7 us -> 13.1 us  [reinitialize(): pl.pallas_call(functools.partial(reinit_kernel, rows, cols), out_shape=ja...]
where the time goes in v6:
time: 43.4 us; the launch traced here: 43.2 us
  Pallas kernels  40.8 us (94%)
  local copies, waits for them, and re-layouts  2.45 us (6%)
    pallas_call x1, Pallas kernels, advance(): pl.pallas_call(functools.partial(advance_kernel, rows, cols, n_gx, n_gy),...  27.6 us
    pallas_call x1, Pallas kernels, reinitialize(): pl.pallas_call(functools.partial(reinit_kernel, rows, cols), out_shape=ja...  13.1 us
    unnamed x6, local copies, waits for them, and re-layouts  2.45 us

profile of v6, /device:TPU:0, one launch (start us, length us, event | category | flops | bytes accessed | tf_op | source)
XLA Modules:
  0.0 43.2 jit_solution(3921376700258994903)
XLA Ops:
  0.0 0.0 copy-start
  0.0 1.2 %copy-done = f32[32,64,128]{2,1,0:T(8,128)S(1)} copy-done((f32[32,64,128]{2,1,0:T(8,128)S(1)}, f32[32,64,128]{2,1,0:T(8,128)}, u32[]{:S(2)}) %copy-start) | copy-done | bytes 1048600
  1.2 0.0 copy-start.1
  1.2 1.2 %copy-done.1 = f32[32,64,128]{2,1,0:T(8,128)S(1)} copy-done((f32[32,64,128]{2,1,0:T(8,128)S(1)}, f32[32,64,128]{2,1,0:T(8,128)}, u32[]{:S(2)}) %copy-start.1) | copy-done | bytes 1048600
  2.5 0.0 copy-start.2
  2.5 27.6 %advance.1.start = f32[2048,128]{1,0:T(8,128)S(1)} custom-call(f32[2048,128]{1,0:T(8,128)S(1)} %bitcast.3, f32[2048,128]{1,0:T(8,128)S(1)} %bitcast.4), custom_call_target="tpu_custom_call" | custom-call | tf_op jit(solution)/shard_map/advance/pallas_call | solution.py:387
  30.1 0.0 copy-done.2
  30.1 13.1 %reinitialize.1 = f32[2048,128]{1,0:T(8,128)} custom-call(f32[2048,128]{1,0:T(8,128)S(1)} %advance.1.start, s32[2,4]{1,0:T(2,128)S(1)} %copy-done.2), custom_call_target="tpu_custom_call" | custom-call | tf_op jit(solution)/shard_map/reinitialize/pallas_call | solution.py:505
Async XLA Ops:
  0.0 1.2 %copy-start = (f32[32,64,128]{2,1,0:T(8,128)S(1)}, f32[32,64,128]{2,1,0:T(8,128)}, u32[]{:S(2)}) copy-start(f32[32,64,128]{2,1,0:T(8,128)} %param.3) | copy-start | bytes 3145732
  1.2 1.2 %copy-start.1 = (f32[32,64,128]{2,1,0:T(8,128)S(1)}, f32[32,64,128]{2,1,0:T(8,128)}, u32[]{:S(2)}) copy-start(f32[32,64,128]{2,1,0:T(8,128)} %param.4) | copy-start | bytes 3145732
  2.5 27.7 %copy-start.2 = (s32[2,4]{1,0:T(2,128)S(1)}, s32[2,4]{1,0:T(2,128)}, u32[]{:S(2)}) copy-start(s32[2,4]{1,0:T(2,128)} %band.1) | copy-start | bytes 100
